TPU v7x, 32 devices: a whole 2x2x4 slice. The times are simulated.
32 devices in a mesh: grp: 2 (over x), tile: 16 (over z, y, core).
Axes of the slice: x: 2, y: 2, z: 4, core: 2. Of those that a mesh axis runs over, the one named last changes fastest.
Arguments:
- latent: float32 [32, 1024, 128], P(None, ('grp', 'tile')), parts along dimension 1, may hold values from -6 to 6
- observed: float32 [32, 1024, 128], P(None, ('grp', 'tile')), parts along dimension 1, may hold values from -6 to 6
- noise: float32 [32, 1024, 128], P(None, ('grp', 'tile')), parts along dimension 1, may hold values from -6 to 6
- cloudy: int32 [128], P(('grp', 'tile')), parts along dimension 0, may hold values from 0 to 1, as said below
- timestep: int32 [2], P('grp'), parts along dimension 0, may hold values from 200 to 800
- pos_embed: bfloat16 [256, 2048], replicated, may hold values from -3 to 3
- embed_w: bfloat16 [128, 2048], replicated, may hold values from -0.5 to 0.5
- mod_w: bfloat16 [256, 6144], P(None, 'tile'), may hold values from -0.375 to 0.375
- wq: bfloat16 [2048, 1024], P('tile')
- wk: bfloat16 [2048, 1024], P('tile')
- wv: bfloat16 [2048, 1024], P('tile'), may hold values from -0.125 to 0.125
- wo: bfloat16 [1024, 2048], P(None, 'tile'), may hold values from -0.1875 to 0.1875
- q_gain: float32 [128], replicated, may hold values from 0.6 to 4.2
- k_gain: float32 [128], replicated, may hold values from 0.6 to 4.2
- out_w: bfloat16 [2048, 128], replicated, may hold values from -0.125 to 0.125
- conv_w: float32 [9, 32, 32], replicated, may hold values from -0.375 to 0.375
Outputs:
- estimate: float32 [32, 1024, 128], P(None, ('grp', 'tile')), parts along dimension 1
- next_latent: float32 [32, 1024, 128], P(None, ('grp', 'tile')), parts along dimension 1
There are 2 independent parts, one for each index of `grp`. A program takes and returns all parts, laid end to end along the dimension named above; an argument that names none is the same for every part. Nothing has to cross between parts.
Inputs may be any that keep to these rules, and one draw needn't show every extreme that they name: Exactly 16 tiles of a part are cloudy; each band of 4 tiles holds at most 3 of them, and some band holds exactly 3.
All inputs are finite; a program needn't handle non-finite values.
Results may differ from a plain program's by a relative error of at most 0.0033.
Values may be sent and summed in bfloat16 or wider, within the bound.
A program may use at most 128 MiB of HBM per device.

v0:
```python
import math

import jax
import jax.numpy as jnp
from jax import lax
from jax.sharding import PartitionSpec as P

HD = 128
PATCH = 2
MAXOWN = 3
TSTEPS = 1000
STRIDE = 20


def padded_2(block, sides, width):
    for axis, dim in sides:
        count = lax.axis_size(axis)
        forward = [(i, i + 1) for i in range(count - 1)]
        backward = [(target, source) for source, target in forward]
        low = lax.ppermute(
            lax.slice_in_dim(block, block.shape[dim] - width, None, axis=dim), axis, forward
        )
        high = lax.ppermute(lax.slice_in_dim(block, 0, width, axis=dim), axis, backward)
        block = jnp.concatenate([low, block, high], axis=dim)
    return block


def plan(step):
    theta = (step / TSTEPS + 0.008) / 1.008 * (math.pi / 2)
    return (jnp.cos(theta), jnp.sin(theta))


def time_features(step, width):
    half = width // 2
    freqs = jnp.exp(-math.log(10000.0) * jnp.arange(half, dtype=jnp.float32) / half)
    angles = step * freqs
    code = jnp.concatenate([jnp.cos(angles), jnp.sin(angles)])[None, :]
    return jax.nn.silu(code).astype(jnp.bfloat16)


def layer_norm(values):
    center = values - jnp.mean(values, axis=-1, keepdims=True)
    spread = jnp.mean(center * center, axis=-1, keepdims=True)
    return center * lax.rsqrt(spread + 1e-06)


def head_norm(proj, gain, count, tokens_tile):
    shaped = proj.reshape(count, tokens_tile, -1, HD)
    scaled = shaped * lax.rsqrt(jnp.mean(shaped * shaped, axis=-1, keepdims=True) + 1e-06)
    return (scaled * gain).astype(jnp.bfloat16)


def band_tiles(band, tile_side):
    channels, band_rows, band_cols = band.shape
    tiles_here = band_cols // (tile_side * PATCH)
    shaped = band.reshape(channels, tile_side, PATCH, tiles_here, tile_side, PATCH)
    return jnp.transpose(shaped, (3, 1, 4, 2, 5, 0)).reshape(
        tiles_here, tile_side * tile_side, PATCH * PATCH * channels
    )


def band_pixels(tiled, tile_side, channels):
    tiles_here = tiled.shape[0]
    shaped = tiled.reshape(tiles_here, tile_side, tile_side, PATCH, PATCH, channels)
    return jnp.transpose(shaped, (5, 1, 3, 0, 2, 4)).reshape(
        channels, tile_side * PATCH, tiles_here * tile_side * PATCH
    )


def add_rows(left, shard_rows):
    return jnp.dot(left, shard_rows, preferred_element_type=jnp.float32)


def denoise(
    chosen,
    embed_w,
    pos_embed,
    shift_vec,
    scale_vec,
    gate_vec,
    wq,
    wk,
    wv,
    wo,
    q_gain,
    k_gain,
    out_w,
):
    count, tokens_tile, token_values = chosen.shape
    row_count = count * tokens_tile
    flat = chosen.reshape(row_count, token_values)
    hidden0 = jnp.dot(flat, embed_w, preferred_element_type=jnp.float32).reshape(
        count, tokens_tile, -1
    )
    hidden0 = (hidden0 + pos_embed.astype(jnp.float32)[None]).reshape(row_count, -1)
    modulated = (layer_norm(hidden0) * (1.0 + scale_vec) + shift_vec).astype(jnp.bfloat16)

    def add_one(shard_rows):
        return add_rows(modulated, shard_rows)

    query_all = add_one(lax.all_gather(wq, "tile", axis=0, tiled=True))
    key_all = add_one(lax.all_gather(wk, "tile", axis=0, tiled=True))
    value_all = add_one(lax.all_gather(wv, "tile", axis=0, tiled=True))
    query_norm = head_norm(query_all, q_gain, count, tokens_tile)
    key_norm = head_norm(key_all, k_gain, count, tokens_tile)
    value_half = value_all.reshape(count, tokens_tile, -1, HD).astype(jnp.bfloat16)
    scores = jnp.einsum(
        "nqhd,nkhd->nhqk", query_norm, key_norm, preferred_element_type=jnp.float32
    ) * HD ** (-0.5)
    peak = jnp.max(scores, axis=-1, keepdims=True)
    expo = jnp.exp(scores - peak)
    probs = (expo / jnp.sum(expo, axis=-1, keepdims=True)).astype(jnp.bfloat16)
    mixed = jnp.einsum("nhqk,nkhd->nqhd", probs, value_half, preferred_element_type=jnp.float32)
    mixed = mixed.astype(jnp.bfloat16).reshape(row_count, -1)
    attn_out = jnp.dot(
        mixed, lax.all_gather(wo, "tile", axis=1, tiled=True), preferred_element_type=jnp.float32
    )
    hidden1 = hidden0 + gate_vec * attn_out
    final = layer_norm(hidden1).astype(jnp.bfloat16)
    eps_pred = jnp.dot(final, out_w, preferred_element_type=jnp.float32).astype(jnp.bfloat16)
    return eps_pred.reshape(count, tokens_tile, token_values)


def on_device(
    latent,
    observed,
    noise,
    cloudy,
    timestep,
    pos_embed,
    embed_w,
    mod_w,
    wq,
    wk,
    wv,
    wo,
    q_gain,
    k_gain,
    out_w,
    conv_w,
):
    channels, band_rows, band_cols = latent.shape
    tile_side = band_rows // PATCH
    tiles_here = band_cols // band_rows
    width = embed_w.shape[1]
    step_now = timestep[0].astype(jnp.float32)
    cos_now, sin_now = plan(step_now)
    cos_prev, sin_prev = plan(step_now - STRIDE)
    time_code = time_features(step_now, mod_w.shape[0])
    local_mod = jnp.dot(time_code, mod_w, preferred_element_type=jnp.float32)
    modulation = lax.all_gather(local_mod, "tile", axis=1, tiled=True)
    shift_vec = modulation[:, :width]
    scale_vec = modulation[:, width : 2 * width]
    gate_vec = modulation[:, 2 * width :]
    tile_tokens = band_tiles(latent.astype(jnp.bfloat16), tile_side)
    order_in = jnp.cumsum(cloudy) - cloudy
    weights_all = (
        embed_w,
        pos_embed,
        shift_vec,
        scale_vec,
        gate_vec,
        wq,
        wk,
        wv,
        wo,
        q_gain,
        k_gain,
        out_w,
    )
    slot_ids = jnp.arange(MAXOWN, dtype=jnp.int32)
    slot_hit = (cloudy[None, :] == 1) & (order_in[None, :] == slot_ids[:, None])
    picked = jnp.sum(
        jnp.where(slot_hit, jnp.arange(tiles_here, dtype=jnp.int32)[None, :], 0), axis=1
    )
    chosen = jnp.take(tile_tokens, picked, axis=0)
    eps_chosen = denoise(chosen, *weights_all)
    eps_back = jnp.take(eps_chosen, jnp.minimum(order_in, MAXOWN - 1), axis=0)
    eps_tiles = jnp.where(cloudy[:, None, None] == 1, eps_back, jnp.zeros_like(eps_back))
    eps_latent = band_pixels(eps_tiles.astype(jnp.float32), tile_side, channels)
    cloud_cols = jnp.repeat(cloudy, band_rows) == 1
    raw_estimate = jnp.where(
        cloud_cols[None, None, :], (latent - sin_now * eps_latent) / cos_now, observed
    )
    padded = padded_2(raw_estimate, (("tile", 1),), 1)
    padded = jnp.pad(padded, ((0, 0), (0, 0), (1, 1)))
    blended = jnp.zeros_like(raw_estimate)
    for row_shift in range(3):
        for col_shift in range(3):
            window = padded[:, row_shift : row_shift + band_rows, col_shift : col_shift + band_cols]
            blended = blended + jnp.einsum(
                "oc,chw->ohw",
                conv_w[3 * row_shift + col_shift],
                window,
                precision=lax.Precision.HIGHEST,
            )
    row_pos = jnp.arange(band_rows) % band_rows
    col_pos = jnp.arange(band_cols) % band_rows
    seam_mask = ((row_pos == 0) | (row_pos == band_rows - 1))[:, None] | (
        (col_pos == 0) | (col_pos == band_rows - 1)
    )[None, :]
    estimate = jnp.where(seam_mask[None], blended, raw_estimate)
    next_latent = cos_prev * estimate + sin_prev * noise
    return (estimate, next_latent)


def solution(mesh):
    placed = (
        P(None, ("grp", "tile"), None),
        P(None, ("grp", "tile"), None),
        P(None, ("grp", "tile"), None),
        P(("grp", "tile")),
        P("grp"),
        P(),
        P(),
        P(None, "tile"),
        P("tile", None),
        P("tile", None),
        P("tile", None),
        P(None, "tile"),
        P(),
        P(),
        P(),
        P(),
    )
    return jax.shard_map(
        on_device,
        mesh=mesh,
        in_specs=placed,
        out_specs=(P(None, ("grp", "tile"), None), P(None, ("grp", "tile"), None)),
        check_vma=False,
    )
```

profile of v0, /device:TPU:1, one launch (start us, length us, event | category | flops | bytes accessed | tf_op | source)
XLA Modules:
  0.0 257.6 jit_solution(8507005595487570797)
XLA Ops:
  12.3 1.1 convolution_bitcast_fusion
  13.6 1.5 copy.77
  15.1 1.1 copy.78
  16.8 1.5 convert_element_type.57
  19.0 23.0 %all-gather.1 = f32[16,1,384]{2,1,0:T(1,128)S(1)} all-gather(f32[1,1,384]{2,1,0:T(1,128)S(1)} %convolution_bitcast_fusion), channel_id=2, replica_groups=mesh['grp'=2,'tile'=16] {'tile'}, dimensions={0}, use_global_device_ids=true | all-gather | bytes 26112 | tf_op jit(solution)/shard_map/all_gather | solution.py:151
  42.1 1.1 fusion.72
  44.0 1.8 copy-done.2
  45.8 2.8 %fusion.4 = bf16[3,256,2048,1]{2,1,3,0:T(8,128)(2,1)} fusion(f32[3,256,2048]{2,1,0:T(8,128)S(1)} %get-tuple-element.22, f32[2048]{0:T(1024)S(1)} %bitcast.119, f32[2048]{0:T(1024)S(1)} %bitcast.118, f32[3,256]{1,0:T(4,128)S(1)} %add_rsqrt_fusion.3, f32[3,256]{1,0:T(4,128)S(1)} %broadcast_multiply_fusion.1), kind=kLoop, calls=%fused_computation.13 | loop fusion | flops 7864320 | bytes 9459712 | tf_op jit(solution)/shard_map/convert_element_type | solution.py:96
  48.7 14.8 %all-gather.11.cloned.1.call-done = bf16[2048,1024]{1,0:T(8,128)(2,1)} async-done(((bf16[128,1024]{1,0:T(8,128)(2,1)}), bf16[2048,1024]{1,0:T(8,128)(2,1)}) %all-gather.11.cloned.1.call-update) | async-done | bytes 4194320 | tf_op jit(solution)/shard_map/all_gather | solution.py:102
  63.5 6.5 %copy.81 = bf16[1024,2048]{1,0:T(8,128)(2,1)} copy(bf16[1024,2048]{0,1:T(8,128)(2,1)} %bitcast.108) | data formatting | bytes 8388608 | tf_op jit(solution)/shard_map/dot_general | solution.py:71
  70.0 44.7 %all-gather.9.cloned.1.call-done = bf16[2048,1024]{1,0:T(8,128)(2,1)} async-done(((bf16[128,1024]{1,0:T(8,128)(2,1)}), bf16[2048,1024]{1,0:T(8,128)(2,1)}) %all-gather.9.cloned.1.call-update) | async-done | bytes 4194320 | tf_op jit(solution)/shard_map/all_gather | solution.py:101
  114.7 6.5 %copy.80 = bf16[1024,2048]{1,0:T(8,128)(2,1)} copy(bf16[1024,2048]{0,1:T(8,128)(2,1)} %bitcast.109) | data formatting | bytes 8388608 | tf_op jit(solution)/shard_map/dot_general | solution.py:71
  121.2 44.7 %all-gather.7.cloned.1.call-done = bf16[2048,1024]{1,0:T(8,128)(2,1)} async-done(((bf16[128,1024]{1,0:T(8,128)(2,1)}), bf16[2048,1024]{1,0:T(8,128)(2,1)}) %all-gather.7.cloned.1.call-update) | async-done | bytes 4194320 | tf_op jit(solution)/shard_map/all_gather | solution.py:103
  166.0 6.5 %copy.79 = bf16[1024,2048]{1,0:T(8,128)(2,1)} copy(bf16[1024,2048]{0,1:T(8,128)(2,1)} %bitcast.110) | data formatting | bytes 8388608 | tf_op jit(solution)/shard_map/dot_general | solution.py:71
  172.4 6.6 %multiply_reduce_fusion.3 = (f32[3,256,8]{1,2,0:T(8,128)S(1)}, f32[3,256,8,128]{1,3,2,0:T(8,128)S(1)}) fusion(bf16[3,256,2048,1]{2,1,3,0:T(8,128)(2,1)} %fusion.4, bf16[8,128,2048,1]{2,1,0,3:T(8,128)(2,1)} %bitcast.113), kind=kOutput, calls=%fused_computation.19 | convolution fusion | flops 3222792192 | bytes 10510336 | tf_op jit(solution)/shard_map/dot_general | solution.py:71
  179.1 3.5 %multiply_reduce_fusion.4 = (f32[3,256,8]{1,2,0:T(8,128)S(1)}, f32[3,256,8,128]{1,3,2,0:T(8,128)S(1)}) fusion(bf16[3,256,2048,1]{2,1,3,0:T(8,128)(2,1)S(1)} %copy-done.4, bf16[8,128,2048,1]{2,1,0,3:T(8,128)(2,1)S(1)} %bitcast.112), kind=kOutput, calls=%fused_computation.21 | convolution fusion | flops 3222792192 | bytes 10510336 | tf_op jit(solution)/shard_map/dot_general | solution.py:71
  182.6 1.3 fusion.11
  183.9 4.3 %fusion.73 = (f32[3,8,256]{2,1,0:T(8,128)S(1)}, f32[3,8,256,256]{2,3,1,0:T(8,128)}) fusion(f32[3,8,256,256]{2,3,1,0:T(8,128)S(1)} %fusion.11), kind=kOutput, calls=%fused_computation.131 | output fusion | flops 6291711 | bytes 12607488 | tf_op jit(solution)/shard_map/sub | solution.py:111
  188.2 10.3 %fusion.18 = bf16[3,256,8,128]{1,3,2,0:T(8,128)(2,1)} fusion(f32[3,8,256,256]{2,3,1,0:T(8,128)} %get-tuple-element.28, f32[3,8,256]{2,1,0:T(8,128)S(1)} %get-tuple-element.27, bf16[3,256,2048,1]{2,1,3,0:T(8,128)(2,1)} %fusion.4, bf16[8,128,2048,1]{2,1,0,3:T(8,128)(2,1)} %bitcast.111), kind=kOutput, calls=%fused_computation.37 | convolution fusion | flops 3628597248 | bytes 15228928 | tf_op jit(solution)/shard_map/nhqk,nkhd->nqhd/dot_general | solution.py:113
  198.5 2.0 copy.86
  200.5 19.2 %all-gather.13.cloned.1.call-done = bf16[1024,2048]{1,0:T(8,128)(2,1)} async-done(((bf16[1024,128]{1,0:T(8,128)(2,1)}), bf16[1024,2048]{1,0:T(8,128)(2,1)}) %all-gather.13.cloned.1.call-update) | async-done | bytes 4194320 | tf_op jit(solution)/shard_map/all_gather | solution.py:116
  219.7 7.0 %fusion.74 = (f32[768]{0:T(1024)S(1)}, f32[768,2048]{1,0:T(8,128)S(1)}) fusion(bf16[1024,2048]{1,0:T(8,128)(2,1)} %all-gather.13.cloned.1.call-done, bf16[96,8,8,128]{3,2,1,0:T(8,128)(2,1)S(1)} %bitcast.115, f32[2048]{0:T(1024)S(1)} %bitcast.120, f32[3,256,2048]{2,1,0:T(8,128)} %copy-done.2), kind=kOutput, calls=%fused_computation.132 | convolution fusion | flops 3225943296 | bytes 18361344 | tf_op jit(solution)/shard_map/dot_general | solution.py:115
  227.8 1.1 fusion.22
  229.9 1.1 multiply_bitcast_fusion
  231.0 1.1 copy.87
  232.7 1.6 copy_select_fusion
  234.4 3.2 %collective-permute-start = (f32[32,1,128]{2,0,1:T(8,128)S(1)}, f32[32,1,128]{2,0,1:T(8,128)S(1)}, u32[]{:S(2)}, u32[]{:S(2)}) collective-permute-start(f32[32,1,128]{2,0,1:T(8,128)S(1)} %get-tuple-element.15), channel_id=1, source_target_pairs={{0,1},{1,2},{2,3},{3,4},{4,5},{5,6},{6,7},{7,8},{8,9},{9,10},{10,1... | collective-permute-start | bytes 49160 | tf_op jit(solution)/shard_map/ppermute | solution.py:20
  237.5 2.2 collective-permute-start.1
  240.0 2.6 %collective-permute-done.1 = f32[32,1,128]{2,0,1:T(8,128)S(1)} collective-permute-done((f32[32,1,128]{2,0,1:T(8,128)S(1)}, f32[32,1,128]{2,0,1:T(8,128)S(1)}, u32[]{:S(2)}, u32[]{:S(2)}) %collective-permute-start.1) | collective-permute-done | bytes 16416 | tf_op jit(solution)/shard_map/ppermute | solution.py:23
  248.0 0.9 fusion.39
  248.9 1.1 copy.92
  250.0 1.1 copy.93
  (69 shorter events, 14.6 us)
Async XLA Ops:
  7.2 34.9 %copy-start = (bf16[128,2048]{1,0:T(8,128)(2,1)S(1)}, bf16[128,2048]{1,0:T(8,128)(2,1)}, u32[]{:S(2)}) copy-start(bf16[128,2048]{1,0:T(8,128)(2,1)} %param.22) | copy-start | bytes 1572868
  7.2 56.3 %all-gather.11.cloned.1.call-start = ((), (), s32[]{:S(2)}) async-start(), calls=%async_computation.2 | async-start | bytes 4456448 | tf_op jit(solution)/shard_map/all_gather | solution.py:102
  7.9 106.8 %all-gather.9.cloned.1.call-start = ((), (), s32[]{:S(2)}) async-start(), calls=%async_computation.1 | async-start | bytes 4456448 | tf_op jit(solution)/shard_map/all_gather | solution.py:101
  8.7 157.3 %all-gather.7.cloned.1.call-start = ((), (), s32[]{:S(2)}) async-start(), calls=%async_computation | async-start | bytes 4456448 | tf_op jit(solution)/shard_map/all_gather | solution.py:103
  9.4 210.3 %all-gather.13.cloned.1.call-start = ((), (), s32[]{:S(2)}) async-start(), calls=%async_computation.3 | async-start | bytes 4456448 | tf_op jit(solution)/shard_map/all_gather | solution.py:116
  43.2 2.7 %copy-start.2 = (f32[3,256,2048]{2,1,0:T(8,128)}, f32[3,256,2048]{2,1,0:T(8,128)S(1)}, u32[]{:S(2)}) copy-start(f32[3,256,2048]{2,1,0:T(8,128)S(1)} %get-tuple-element.22) | copy-start | bytes 18874372
  172.4 6.7 %copy-start.3 = (bf16[1024,2048]{1,0:T(8,128)(2,1)S(1)}, bf16[1024,2048]{1,0:T(8,128)(2,1)}, u32[]{:S(2)}) copy-start(bf16[1024,2048]{1,0:T(8,128)(2,1)} %copy.80) | copy-start | bytes 12582916
  172.4 6.7 %copy-start.4 = (bf16[3,256,2048,1]{2,1,3,0:T(8,128)(2,1)S(1)}, bf16[3,256,2048,1]{2,1,3,0:T(8,128)(2,1)}, u32[]{:S(2)}) copy-start(bf16[3,256,2048,1]{2,1,3,0:T(8,128)(2,1)} %fusion.4) | copy-start | bytes 9437188
  179.1 3.5 %copy-start.9 = (f32[128]{0:T(128)S(1)}, f32[128]{0:T(128)}, u32[]{:S(2)}) copy-start(f32[128]{0:T(128)} %param.29) | copy-start | bytes 1540
  179.1 3.5 %copy-start.10 = (f32[128]{0:T(128)S(1)}, f32[128]{0:T(128)}, u32[]{:S(2)}) copy-start(f32[128]{0:T(128)} %param.28) | copy-start | bytes 1540
  226.7 1.0 copy-start.7
  230.9 1.8 copy-start.5
  232.1 10.8 %copy-start.8 = (f32[9,32,32]{2,1,0:T(8,128)S(1)}, f32[9,32,32]{2,1,0:T(8,128)}, u32[]{:S(2)}) copy-start(f32[9,32,32]{2,1,0:T(8,128)} %param.31) | copy-start | bytes 110596
  234.4 5.6 %collective-permute-start = (f32[32,1,128]{2,0,1:T(8,128)S(1)}, f32[32,1,128]{2,0,1:T(8,128)S(1)}, u32[]{:S(2)}, u32[]{:S(2)}) collective-permute-start(f32[32,1,128]{2,0,1:T(8,128)S(1)} %get-tuple-element.15), channel_id=1, source_target_pairs={{0,1},{1,2},{2,3},{3,4},{4,5},{5,6},{6,7},{7,8},{8,9},{9,10},{10,1... | collective-permute-start | bytes 49160 | tf_op jit(solution)/shard_map/ppermute | solution.py:20
  237.5 5.1 %collective-permute-start.1 = (f32[32,1,128]{2,0,1:T(8,128)S(1)}, f32[32,1,128]{2,0,1:T(8,128)S(1)}, u32[]{:S(2)}, u32[]{:S(2)}) collective-permute-start(f32[32,1,128]{2,0,1:T(8,128)S(1)} %get-tuple-element.16), channel_id=1, source_target_pairs={{1,0},{2,1},{3,2},{4,3},{5,4},{6,5},{7,6},{8,7},{9,8},{10,9},{11,1... | collective-permute-start | bytes 49160 | tf_op jit(solution)/shard_map/ppermute | solution.py:23
  245.5 2.5 copy-start.6
  247.4 3.7 %copy-start.1 = (bf16[128,2048]{1,0:T(8,128)(2,1)S(1)}, bf16[128,2048]{1,0:T(8,128)(2,1)}, u32[]{:S(2)}) copy-start(bf16[128,2048]{1,0:T(8,128)(2,1)} %param.22) | copy-start | bytes 1572868
Sparse Core Ops, SparseCore 0:
  10.2 53.2 all-gather.10
  65.6 49.0 all-gather.8
  116.9 49.0 all-gather.6
  168.0 51.7 all-gather.12
where the time goes:
time: 258 us
  waiting for transfers between devices  129 us (50%)
  matrix products  37.7 us (15%)
  local copies, waits for them, and re-layouts  32.5 us (13%)
  blocking collectives  23 us (9%)
  between operations  15.2 us (6%)
  other arithmetic  15 us (6%)
  starting transfers between devices  5.5 us (2%)
    all_gather x1, waiting for transfers between devices, denoise(): value_all = add_one(lax.all_gather(wv, 'tile', axis=0, tiled=True))  44.7 us
    all_gather x1, waiting for transfers between devices, denoise(): query_all = add_one(lax.all_gather(wq, 'tile', axis=0, tiled=True))  44.7 us
    all_gather x1, blocking collectives, on_device(): modulation = lax.all_gather(local_mod, 'tile', axis=1, tiled=True)  23 us
    dot_general x3, local copies, waits for them, and re-layouts, add_rows(): return jnp.dot(left, shard_rows, preferred_element_type=jnp.float32)  19.5 us
    all_gather x1, waiting for transfers between devices, denoise(): lax.all_gather(wo, 'tile', axis=1, tiled=True)  19.2 us
    all_gather x1, waiting for transfers between devices, denoise(): key_all = add_one(lax.all_gather(wk, 'tile', axis=0, tiled=True))  14.8 us
    dot_general x1, matrix products, denoise(): jnp.einsum('nhqk,nkhd->nqhd', probs, value_half, preferred_element_type=j...  10.3 us
    dot_general x2, matrix products, add_rows(): return jnp.dot(left, shard_rows, preferred_element_type=jnp.float32)  10.1 us
  transfers between devices with their start and end apart: 6, of which 5 were waited for; matrix products, arithmetic and copies ran while one was open for 23% of the time, Pallas kernels for 0%

commit v1 on v0

--- a/solution.py
+++ b/solution.py
@@ -3,6 +3,8 @@
 import jax
 import jax.numpy as jnp
 from jax import lax
+from jax.experimental import pallas as pl
+from jax.experimental.pallas import tpu as pltpu
 from jax.sharding import PartitionSpec as P
 
 HD = 128
@@ -38,87 +40,98 @@
     return jax.nn.silu(code).astype(jnp.bfloat16)
 
 
-def layer_norm(values):
-    center = values - jnp.mean(values, axis=-1, keepdims=True)
-    spread = jnp.mean(center * center, axis=-1, keepdims=True)
-    return center * lax.rsqrt(spread + 1e-06)
-
-
-def head_norm(proj, gain, count, tokens_tile):
-    shaped = proj.reshape(count, tokens_tile, -1, HD)
-    scaled = shaped * lax.rsqrt(jnp.mean(shaped * shaped, axis=-1, keepdims=True) + 1e-06)
-    return (scaled * gain).astype(jnp.bfloat16)
-
-
 def band_tiles(band, tile_side):
     channels, band_rows, band_cols = band.shape
     tiles_here = band_cols // (tile_side * PATCH)
     shaped = band.reshape(channels, tile_side, PATCH, tiles_here, tile_side, PATCH)
-    return jnp.transpose(shaped, (3, 1, 4, 2, 5, 0)).reshape(
-        tiles_here, tile_side * tile_side, PATCH * PATCH * channels
+    return jnp.transpose(shaped, (3, 2, 5, 0, 1, 4)).reshape(
+        tiles_here, PATCH * PATCH * channels, tile_side * tile_side
     )
 
 
 def band_pixels(tiled, tile_side, channels):
     tiles_here = tiled.shape[0]
-    shaped = tiled.reshape(tiles_here, tile_side, tile_side, PATCH, PATCH, channels)
-    return jnp.transpose(shaped, (5, 1, 3, 0, 2, 4)).reshape(
+    shaped = tiled.reshape(tiles_here, PATCH, PATCH, channels, tile_side, tile_side)
+    return jnp.transpose(shaped, (3, 4, 1, 0, 5, 2)).reshape(
         channels, tile_side * PATCH, tiles_here * tile_side * PATCH
     )
 
 
-def add_rows(left, shard_rows):
-    return jnp.dot(left, shard_rows, preferred_element_type=jnp.float32)
-
-
-def denoise(
-    chosen,
-    embed_w,
-    pos_embed,
-    shift_vec,
-    scale_vec,
-    gate_vec,
-    wq,
-    wk,
-    wv,
-    wo,
-    q_gain,
-    k_gain,
-    out_w,
-):
-    count, tokens_tile, token_values = chosen.shape
-    row_count = count * tokens_tile
-    flat = chosen.reshape(row_count, token_values)
-    hidden0 = jnp.dot(flat, embed_w, preferred_element_type=jnp.float32).reshape(
-        count, tokens_tile, -1
-    )
-    hidden0 = (hidden0 + pos_embed.astype(jnp.float32)[None]).reshape(row_count, -1)
-    modulated = (layer_norm(hidden0) * (1.0 + scale_vec) + shift_vec).astype(jnp.bfloat16)
-
-    def add_one(shard_rows):
-        return add_rows(modulated, shard_rows)
-
-    query_all = add_one(lax.all_gather(wq, "tile", axis=0, tiled=True))
-    key_all = add_one(lax.all_gather(wk, "tile", axis=0, tiled=True))
-    value_all = add_one(lax.all_gather(wv, "tile", axis=0, tiled=True))
-    query_norm = head_norm(query_all, q_gain, count, tokens_tile)
-    key_norm = head_norm(key_all, k_gain, count, tokens_tile)
-    value_half = value_all.reshape(count, tokens_tile, -1, HD).astype(jnp.bfloat16)
-    scores = jnp.einsum(
-        "nqhd,nkhd->nhqk", query_norm, key_norm, preferred_element_type=jnp.float32
-    ) * HD ** (-0.5)
-    peak = jnp.max(scores, axis=-1, keepdims=True)
-    expo = jnp.exp(scores - peak)
-    probs = (expo / jnp.sum(expo, axis=-1, keepdims=True)).astype(jnp.bfloat16)
-    mixed = jnp.einsum("nhqk,nkhd->nqhd", probs, value_half, preferred_element_type=jnp.float32)
-    mixed = mixed.astype(jnp.bfloat16).reshape(row_count, -1)
-    attn_out = jnp.dot(
-        mixed, lax.all_gather(wo, "tile", axis=1, tiled=True), preferred_element_type=jnp.float32
-    )
-    hidden1 = hidden0 + gate_vec * attn_out
-    final = layer_norm(hidden1).astype(jnp.bfloat16)
-    eps_pred = jnp.dot(final, out_w, preferred_element_type=jnp.float32).astype(jnp.bfloat16)
-    return eps_pred.reshape(count, tokens_tile, token_values)
+def centered(values):
+    values = values.astype(jnp.float32)
+    return values - jnp.mean(values, axis=-1, keepdims=True)
+
+
+def norm_rows(values):
+    center = values - jnp.mean(values, axis=0, keepdims=True)
+    spread = jnp.mean(center * center, axis=0, keepdims=True)
+    return center, lax.rsqrt(spread + 1e-06)
+
+
+def denoise_kernel(tok_ref, fold_ref, wo_ref, emb_ref, pos_ref, gate_ref, out_w_ref, qg_ref, kg_ref, eps_ref, mix_ref):
+    tokens = tok_ref[0]
+    token_count = tokens.shape[1]
+    per = fold_ref.shape[2]
+    group = HD // per
+    heads = mix_ref.shape[0] // HD
+    h0 = jnp.dot(emb_ref[...], tokens, preferred_element_type=jnp.float32) + pos_ref[...].astype(jnp.float32)
+    _, rstd = norm_rows(h0)
+
+    def project(kind, head):
+        block = fold_ref[pl.ds(head * group, group), kind].reshape(HD, fold_ref.shape[3])
+        base = block[:, :token_count].astype(jnp.float32)
+        own = jnp.dot(block[:, token_count : token_count + tokens.shape[0]], tokens, preferred_element_type=jnp.float32)
+        last = token_count + tokens.shape[0]
+        return (own + base) * rstd + block[:, last : last + 1].astype(jnp.float32)
+
+    def head_norm(proj, gain):
+        spread = jnp.mean(proj * proj, axis=0, keepdims=True)
+        return (proj * lax.rsqrt(spread + 1e-06) * gain).astype(jnp.bfloat16)
+
+    for head in range(heads):
+        query = head_norm(project(0, head), qg_ref[...])
+        key = head_norm(project(1, head), kg_ref[...])
+        value = project(2, head).astype(jnp.bfloat16)
+        scores = lax.dot_general(key, query, (((0,), (0,)), ((), ())), preferred_element_type=jnp.float32) * HD ** (-0.5)
+        expo = jnp.exp(scores - jnp.max(scores, axis=0, keepdims=True))
+        probs = (expo * (1.0 / jnp.sum(expo, axis=0, keepdims=True))).astype(jnp.bfloat16)
+        mixed = jnp.dot(value, probs, preferred_element_type=jnp.float32)
+        mix_ref[head * HD : (head + 1) * HD, :] = mixed.astype(jnp.bfloat16)
+    attn = jnp.dot(wo_ref[...], mix_ref[...], preferred_element_type=jnp.float32)
+    center, rstd1 = norm_rows(h0 + gate_ref[...] * attn)
+    final = (center * rstd1).astype(jnp.bfloat16)
+    eps_ref[0] = jnp.dot(out_w_ref[...], final, preferred_element_type=jnp.float32).astype(jnp.bfloat16)
+
+
+def denoise(chosen, embed_w, pos_embed, shift_vec, scale_vec, gate_vec, wq, wk, wv, wo, q_gain, k_gain, out_w):
+    parts = lax.axis_size("tile")
+    tiles, token_values, token_count = chosen.shape
+    width = embed_w.shape[1]
+    inner = wq.shape[1]
+    per = inner // parts
+    rows = wq.shape[0]
+    stacked = jnp.stack([wq, wk, wv], axis=1).reshape(rows, 3, parts, per)
+    chunks = jnp.transpose(stacked, (2, 0, 1, 3)).reshape(parts, rows, 3 * per)
+    mine = lax.all_to_all(chunks, "tile", 0, 0, tiled=True).reshape(width, 3 * per)
+    wo_t = lax.all_gather(wo.T, "tile", axis=0, tiled=True)
+    folded = jnp.concatenate([centered(pos_embed), centered(embed_w)], axis=0) * (1.0 + scale_vec)
+    pad = -(token_count + token_values + 1) % HD
+    left = jnp.concatenate([folded, shift_vec, jnp.zeros((pad, width), jnp.float32)], axis=0).astype(jnp.bfloat16)
+    fold = lax.dot_general(mine, left, (((0,), (1,)), ((), ())), preferred_element_type=jnp.float32)
+    fold = fold.astype(jnp.bfloat16).reshape(1, 3, per, left.shape[0])
+    fold_all = lax.all_gather(fold, "tile", axis=0, tiled=True)
+    args = (chosen, fold_all, wo_t, embed_w.T, pos_embed.T, gate_vec.reshape(-1, 1), out_w.T, q_gain.reshape(-1, 1), k_gain.reshape(-1, 1))
+    whole = [pl.BlockSpec(memory_space=pltpu.VMEM)] * (len(args) - 1)
+    block = pl.BlockSpec((1, token_values, token_count), lambda i: (i, 0, 0))
+    return pl.pallas_call(
+        denoise_kernel,
+        grid=(tiles,),
+        out_shape=jax.ShapeDtypeStruct(chosen.shape, jnp.bfloat16),
+        in_specs=[block] + whole,
+        out_specs=block,
+        scratch_shapes=[pltpu.VMEM((inner, token_count), jnp.bfloat16)],
+        compiler_params=pltpu.CompilerParams(vmem_limit_bytes=48 * 1024 * 1024),
+    )(*args)
 
 
 def on_device(

time: 258 us -> 209 us (0.81)
  waiting for transfers between devices: 129 us -> 83 us
  matrix products: 37.7 us -> 8.67 us
  Pallas kernels: 0 us -> 27 us
  other arithmetic: 15 us -> 7.23 us
  starting transfers between devices: 5.5 us -> 12.1 us
  local copies, waits for them, and re-layouts: 32.5 us -> 26.3 us
  blocking collectives: 23 us -> 27.8 us
    all_gather x4 -> x2, waiting for transfers between devices: 123 us -> 80.2 us  [the longest x1 52.1 us: denoise(): wo_t = lax.all_gather(wo.T, 'tile', axis=0, tiled=True)]
    dot_general x7 -> x1, matrix products: 30.8 us -> 2.74 us  [denoise(): lax.dot_general(mine, left, (((0,), (1,)), ((), ())), preferred_element_t...]
    pallas_call x0 -> x1, Pallas kernels: none -> 27 us  [denoise(): pl.pallas_call(denoise_kernel, grid=(tiles,), out_shape=jax.ShapeDtypeStr...]
    dot_general x3 -> x0, local copies, waits for them, and re-layouts: 19.5 us -> none  [add_rows(): return jnp.dot(left, shard_rows, preferred_element_type=jnp.float32)]
    unnamed x25 -> x44, local copies, waits for them, and re-layouts: 5.88 us -> 14.6 us
    all_to_all x0 -> x1, starting transfers between devices: none -> 7.48 us  [denoise(): lax.all_to_all(chunks, 'tile', 0, 0, tiled=True).reshape(width, 3 * per)]
    all_gather x1, blocking collectives: 23 us -> 27.8 us  [on_device(): modulation = lax.all_gather(local_mod, 'tile', axis=1, tiled=True)]
    convert_element_type x2 -> x0, other arithmetic: 4.29 us -> none  [the longest x1 2.83 us: denoise(): (layer_norm(hidden0) * (1.0 + scale_vec) + shift_vec).astype(jnp.bfloat16)]
  transfers between devices with their start and end apart: 6 -> 5, of which waited for: 5 -> 3; matrix products, arithmetic and copies ran while one was open for 23% -> 8% of each run, Pallas kernels for 0% -> 0%
where the time goes in v1:
time: 209 us; the launch traced here: 207 us
  waiting for transfers between devices  83 us (40%)
  blocking collectives  27.8 us (13%)
  Pallas kernels  27 us (13%)
  local copies, waits for them, and re-layouts  26.3 us (13%)
  between operations  15.5 us (7%)
  starting transfers between devices  12.1 us (6%)
  matrix products  8.67 us (4%)
  other arithmetic  7.23 us (3%)
    all_gather x1, waiting for transfers between devices, denoise(): wo_t = lax.all_gather(wo.T, 'tile', axis=0, tiled=True)  52.1 us
    all_gather x1, waiting for transfers between devices, denoise(): fold_all = lax.all_gather(fold, 'tile', axis=0, tiled=True)  28 us
    all_gather x1, blocking collectives, on_device(): modulation = lax.all_gather(local_mod, 'tile', axis=1, tiled=True)  27.8 us
    pallas_call x1, Pallas kernels, denoise(): pl.pallas_call(denoise_kernel, grid=(tiles,), out_shape=jax.ShapeDtypeStr...  27 us
    unnamed x44, local copies, waits for them, and re-layouts  14.6 us
    all_to_all x1, starting transfers between devices, denoise(): lax.all_to_all(chunks, 'tile', 0, 0, tiled=True).reshape(width, 3 * per)  7.48 us
    dot_general x9, matrix products, on_device(): jnp.einsum('oc,chw->ohw', conv_w[3 * row_shift + col_shift], window, prec...  5.79 us
  transfers between devices with their start and end apart: 5, of which 3 were waited for; matrix products, arithmetic and copies ran while one was open for 8% of the time, Pallas kernels for 0%

profile of v1, /device:TPU:1, one launch (start us, length us, event | category | flops | bytes accessed | tf_op | source)
XLA Modules:
  0.0 207.5 jit_solution(1504059347578167125)
XLA Ops:
  7.2 1.2 copy.100
  8.3 1.1 copy.101
  9.5 1.1 copy.102
  10.7 1.0 copy.103
  11.7 7.5 %all-to-all-start = ((bf16[16,128,192]{1,2,0:T(8,128)(2,1)}), bf16[16,128,192]{1,2,0:T(8,128)(2,1)}, u32[]{:S(2)}, u32[]{:S(2)}) async-start(bf16[16,128,192]{1,2,0:T(8,128)(2,1)} %bitcast.11), calls=%async_computation | async-start | bytes 1572864 | tf_op jit(solution)/shard_map/all_to_all | solution.py:115
  20.6 27.8 %all-gather.1 = f32[16,1,384]{2,1,0:T(1,128)S(1)} all-gather(f32[1,1,384]{2,1,0:T(1,128)S(1)} %convolution_bitcast_fusion), channel_id=2, replica_groups=mesh['grp'=2,'tile'=16] {'tile'}, dimensions={0}, use_global_device_ids=true | all-gather | bytes 26112 | tf_op jit(solution)/shard_map/all_gather | solution.py:164
  49.1 2.7 %fusion.9 = bf16[192,512]{1,0:T(8,128)(2,1)} fusion(bf16[1,2048]{1,0:T(2,128)(2,1)S(1)} %slice.161, bf16[384,2048]{1,0:T(8,128)(2,1)S(1)} %fusion, bf16[512]{0:T(512)(128)(2,1)S(1)} %pad.14.clone, bf16[16,128,192]{1,2,0:T(8,128)(2,1)} %all-to-all-done), kind=kOutput, calls=%fused_computation.28 | convolution fusion | flops 409042944 | bytes 2561024 | tf_op jit(solution)/shard_map/dot_general | solution.py:120
  52.1 1.8 copy.105
  54.9 1.4 copy.97
  56.4 2.4 %copy.98 = bf16[4,2,2,32,16,16]{3,2,1,5,4,0:T(2,128)(2,1)S(1)} copy(bf16[4,2,2,32,16,16]{3,2,5,0,1,4:T(2,128)(2,1)} %bitcast.94) | data formatting | bytes 524288 | tf_op jit(solution)/shard_map/transpose | solution.py:47
  59.3 0.9 copy.99
  60.5 1.3 copy.108
  61.8 0.7 copy.110.qg_ref
  62.5 0.7 copy.111.kg_ref
  64.8 1.5 gather_fusion
  68.1 0.8 broadcast_select_fusion.2.tok_ref
  68.9 28.0 %all-gather.5.cloned.1.call-done.fold_ref = bf16[16,3,64,512]{3,2,1,0:T(8,128)(2,1)} async-done(((bf16[1,3,64,512]{3,2,1,0:T(8,128)(2,1)}), bf16[16,3,64,512]{3,2,1,0:T(8,128)(2,1)}) %all-gather.5.cloned.1.call-update) | async-done | bytes 3145744 | tf_op jit(solution)/shard_map/all_gather | solution.py:122
  96.9 52.1 %all-gather.7.cloned.1.call-done.wo_ref = bf16[2048,1024]{1,0:T(8,128)(2,1)} async-done(((bf16[128,1024]{1,0:T(8,128)(2,1)}), bf16[2048,1024]{1,0:T(8,128)(2,1)}) %all-gather.7.cloned.1.call-update) | async-done | bytes 4194320 | tf_op jit(solution)/shard_map/all_gather | solution.py:116
  149.0 0.9 copy-done.1
  150.0 0.8 copy-done.2
  150.8 0.8 copy-done.3
  151.6 27.0 %shard_map.167 = bf16[3,128,256]{2,1,0:T(8,128)(2,1)S(1)} custom-call(bf16[3,128,256]{2,1,0:T(8,128)(2,1)S(1)} %copy-done.1, bf16[16,3,64,512]{3,2,1,0:T(8,128)(2,1)} %all-gather.5.cloned.1.call-done.fold_ref, bf16[2048,1024]{1,0:T(8,128)(2,1)} %all-gather.7.cloned.1.call-done.wo_ref, bf16[2048,128]{1,0:T(8,128)(2,1)S(1)} %bitcast.91, ...), custom_call_target="tpu_custom_call" | custom-call | tf_op jit(solution)/shard_map/pallas_call | solution.py:126
  179.8 1.1 multiply_bitcast_fusion
  180.9 1.1 copy.113
  183.1 1.7 copy_select_fusion
  184.8 2.3 %collective-permute-start = (f32[32,1,128]{2,0,1:T(8,128)S(1)}, f32[32,1,128]{2,0,1:T(8,128)S(1)}, u32[]{:S(2)}, u32[]{:S(2)}) collective-permute-start(f32[32,1,128]{2,0,1:T(8,128)S(1)} %get-tuple-element.15), channel_id=1, source_target_pairs={{0,1},{1,2},{2,3},{3,4},{4,5},{5,6},{6,7},{7,8},{8,9},{9,10},{10,1... | collective-permute-start | bytes 49160 | tf_op jit(solution)/shard_map/ppermute | solution.py:22
  187.1 2.0 collective-permute-start.1
  189.4 2.8 %collective-permute-done.1 = f32[32,1,128]{2,0,1:T(8,128)S(1)} collective-permute-done((f32[32,1,128]{2,0,1:T(8,128)S(1)}, f32[32,1,128]{2,0,1:T(8,128)S(1)}, u32[]{:S(2)}, u32[]{:S(2)}) %collective-permute-start.1) | collective-permute-done | bytes 16416 | tf_op jit(solution)/shard_map/ppermute | solution.py:25
  194.4 0.7 convolution_add_fusion.5
  197.5 0.9 fusion.30
  198.4 1.1 copy.118
  199.5 1.1 copy.119
  (82 shorter events, 13.7 us)
Async XLA Ops:
  7.2 13.3 %copy-start = (bf16[256,384]{1,0:T(8,128)(2,1)S(1)}, bf16[256,384]{1,0:T(8,128)(2,1)}, u32[]{:S(2)}) copy-start(bf16[256,384]{1,0:T(8,128)(2,1)} %param.23) | copy-start | bytes 589828
  10.7 9.2 %copy-start.4 = (bf16[256,2048]{1,0:T(8,128)(2,1)S(1)}, bf16[256,2048]{1,0:T(8,128)(2,1)}, u32[]{:S(2)}) copy-start(bf16[256,2048]{1,0:T(8,128)(2,1)} %param.21) | copy-start | bytes 3145732
  11.7 8.5 %copy-start.5 = (bf16[128,2048]{1,0:T(8,128)(2,1)S(1)}, bf16[128,2048]{1,0:T(8,128)(2,1)}, u32[]{:S(2)}) copy-start(bf16[128,2048]{1,0:T(8,128)(2,1)} %param.22) | copy-start | bytes 1572868
  11.7 37.4 %all-to-all-start = ((bf16[16,128,192]{1,2,0:T(8,128)(2,1)}), bf16[16,128,192]{1,2,0:T(8,128)(2,1)}, u32[]{:S(2)}, u32[]{:S(2)}) async-start(bf16[16,128,192]{1,2,0:T(8,128)(2,1)} %bitcast.11), calls=%async_computation | async-start | bytes 1572864 | tf_op jit(solution)/shard_map/all_to_all | solution.py:115
  19.2 77.7 %all-gather.5.cloned.1.call-start = ((), (), s32[]{:S(2)}) async-start(), calls=%async_computation.1 | async-start | bytes 3342336 | tf_op jit(solution)/shard_map/all_gather | solution.py:122
  51.8 97.2 %all-gather.7.cloned.1.call-start = ((), (), s32[]{:S(2)}) async-start(), calls=%async_computation.2 | async-start | bytes 4456448 | tf_op jit(solution)/shard_map/all_gather | solution.py:116
  53.9 1.0 copy-start.6
  59.2 2.5 %copy-start.10 = (f32[128]{0:T(128)S(1)}, f32[128]{0:T(128)}, u32[]{:S(2)}) copy-start(f32[128]{0:T(128)} %param.28) | copy-start | bytes 1540
  59.3 3.3 %copy-start.11 = (f32[128]{0:T(128)S(1)}, f32[128]{0:T(128)}, u32[]{:S(2)}) copy-start(f32[128]{0:T(128)} %param.29) | copy-start | bytes 1540
  59.3 4.0 %copy-start.14 = (s32[4]{0:T(128)S(1)}, s32[4]{0:T(128)}, u32[]{:S(2)}) copy-start(s32[4]{0:T(128)} %param.19) | copy-start | bytes 52
  64.2 0.6 copy-start.16
  149.0 0.9 copy-start.1
  150.0 0.8 copy-start.2
  150.8 0.8 copy-start.3
  182.0 1.0 copy-start.7
  182.0 1.0 copy-start.15
  183.1 6.0 %copy-start.12 = (pred[128]{0:T(512)(128)(4,1)S(1)}, pred[128]{0:T(512)(128)(4,1)}, u32[]{:S(2)}) copy-start(pred[128]{0:T(512)(128)(4,1)} %compare_or_fusion) | copy-start | bytes 388
  183.1 6.0 %copy-start.13 = (pred[32]{0:T(512)(128)(4,1)S(1)}, pred[32]{0:T(512)(128)(4,1)}, u32[]{:S(2)}) copy-start(pred[32]{0:T(512)(128)(4,1)} %compare_or_fusion.1) | copy-start | bytes 100
  183.1 9.4 %copy-start.9 = (f32[9,32,32]{2,1,0:T(8,128)S(1)}, f32[9,32,32]{2,1,0:T(8,128)}, u32[]{:S(2)}) copy-start(f32[9,32,32]{2,1,0:T(8,128)} %param.31) | copy-start | bytes 110596
  184.8 4.6 %collective-permute-start = (f32[32,1,128]{2,0,1:T(8,128)S(1)}, f32[32,1,128]{2,0,1:T(8,128)S(1)}, u32[]{:S(2)}, u32[]{:S(2)}) collective-permute-start(f32[32,1,128]{2,0,1:T(8,128)S(1)} %get-tuple-element.15), channel_id=1, source_target_pairs={{0,1},{1,2},{2,3},{3,4},{4,5},{5,6},{6,7},{7,8},{8,9},{9,10},{10,1... | collective-permute-start | bytes 49160 | tf_op jit(solution)/shard_map/ppermute | solution.py:22
  187.1 5.1 %collective-permute-start.1 = (f32[32,1,128]{2,0,1:T(8,128)S(1)}, f32[32,1,128]{2,0,1:T(8,128)S(1)}, u32[]{:S(2)}, u32[]{:S(2)}) collective-permute-start(f32[32,1,128]{2,0,1:T(8,128)S(1)} %get-tuple-element.16), channel_id=1, source_target_pairs={{1,0},{2,1},{3,2},{4,3},{5,4},{6,5},{7,6},{8,7},{9,8},{10,9},{11,1... | collective-permute-start | bytes 49160 | tf_op jit(solution)/shard_map/ppermute | solution.py:25
  196.2 1.3 copy-start.8
Sparse Core Ops, SparseCore 0:
  51.9 44.9 all-gather.4
  99.6 49.3 all-gather.6

commit v2 on v1

--- a/solution.py
+++ b/solution.py
@@ -1,3 +1,4 @@
+import functools
 import math
 
 import jax
@@ -62,49 +63,176 @@
     return values - jnp.mean(values, axis=-1, keepdims=True)
 
 
+LO = 4
+
+
+def send(src, dst, sems, slot, target):
+    copy = pltpu.make_async_remote_copy(
+        src_ref=src,
+        dst_ref=dst,
+        send_sem=sems[0].at[slot],
+        recv_sem=sems[1].at[slot],
+        device_id={"tile": target},
+        device_id_type=pl.DeviceIdType.MESH,
+    )
+    copy.start()
+    return copy
+
+
+def greet(targets):
+    barrier = pltpu.get_barrier_semaphore()
+    for target in targets:
+        pl.semaphore_signal(barrier, inc=1, device_id={"tile": target}, device_id_type=pl.DeviceIdType.MESH)
+    pl.semaphore_wait(barrier, len(targets))
+
+
+def pair(count):
+    return [pltpu.SemaphoreType.DMA((count,)), pltpu.SemaphoreType.DMA((count,))]
+
+
+def spread_kernel(parts, mod_ref, chunk_ref, wo_ref, mods_ref, mine_ref, line_ref, ms, mr, cs, cr, ws, wr):
+    me = lax.axis_index("tile")
+    level, lane = me // LO, lax.rem(me, LO)
+    levels = parts // LO
+    others = [lax.rem(me + k, parts) for k in range(1, parts)]
+    greet(others)
+    copies = []
+    for k, target in enumerate(others):
+        copies.append(send(mod_ref, mods_ref.at[me], (ms, mr), k, target))
+    for k, target in enumerate(others):
+        copies.append(send(chunk_ref.at[target], mine_ref.at[me], (cs, cr), k, target))
+    for k in range(1, levels):
+        target = lax.rem(level + k, levels) * LO + lane
+        copies.append(send(wo_ref, line_ref.at[level], (ws, wr), k - 1, target))
+    mods_ref[me] = mod_ref[...]
+    mine_ref[me] = chunk_ref[me]
+    line_ref[level] = wo_ref[...]
+    for copy in copies:
+        copy.wait_recv()
+    for copy in copies:
+        copy.wait_send()
+
+
 def norm_rows(values):
     center = values - jnp.mean(values, axis=0, keepdims=True)
     spread = jnp.mean(center * center, axis=0, keepdims=True)
     return center, lax.rsqrt(spread + 1e-06)
 
 
-def denoise_kernel(tok_ref, fold_ref, wo_ref, emb_ref, pos_ref, gate_ref, out_w_ref, qg_ref, kg_ref, eps_ref, mix_ref):
-    tokens = tok_ref[0]
-    token_count = tokens.shape[1]
-    per = fold_ref.shape[2]
+def denoise_kernel(
+    parts,
+    tok_ref,
+    fold_ref,
+    line_ref,
+    emb_ref,
+    pos_ref,
+    gate_ref,
+    out_w_ref,
+    qg_ref,
+    kg_ref,
+    eps_ref,
+    all_ref,
+    wo_ref,
+    h0_ref,
+    mix_ref,
+    fzs,
+    fzr,
+    fys,
+    fyr,
+    fcs,
+    fcr,
+    wys,
+    wyr,
+    wcs,
+    wcr,
+):
+    me = lax.axis_index("tile")
+    level, lane = me // LO, lax.rem(me, LO)
+    levels = parts // LO
+    side = lax.rem(lane + 2, LO)
+    twin = lane + 1 - 2 * lax.rem(lane, 2)
+    line = [lax.rem(level + k, levels) * LO + lane for k in range(1, levels)]
+    beside, mate = level * LO + side, level * LO + twin
+    greet(line + [beside, mate])
+
+    sends = []
+    z_copies = [send(fold_ref, all_ref.at[me], (fzs, fzr), k, target) for k, target in enumerate(line)]
+    all_ref[me] = fold_ref[...]
+    y_copies = [send(fold_ref, all_ref.at[me], (fys, fyr), 0, beside)]
+    c_copies = [send(fold_ref, all_ref.at[me], (fcs, fcr), 0, mate)]
+    wy_copies, wc_copies = [], []
+    for k in range(levels):
+        at = lax.rem(level + levels - k, levels)
+        slot = at * LO + lane
+        wy_copies.append(send(line_ref.at[at], wo_ref.at[slot], (wys, wyr), k, beside))
+        wc_copies.append(send(line_ref.at[at], wo_ref.at[slot], (wcs, wcr), k, mate))
+        wo_ref[slot] = line_ref[at]
+
+    tiles, token_values, token_count = tok_ref.shape
+    per = fold_ref.shape[1]
     group = HD // per
-    heads = mix_ref.shape[0] // HD
-    h0 = jnp.dot(emb_ref[...], tokens, preferred_element_type=jnp.float32) + pos_ref[...].astype(jnp.float32)
-    _, rstd = norm_rows(h0)
-
-    def project(kind, head):
-        block = fold_ref[pl.ds(head * group, group), kind].reshape(HD, fold_ref.shape[3])
-        base = block[:, :token_count].astype(jnp.float32)
-        own = jnp.dot(block[:, token_count : token_count + tokens.shape[0]], tokens, preferred_element_type=jnp.float32)
-        last = token_count + tokens.shape[0]
-        return (own + base) * rstd + block[:, last : last + 1].astype(jnp.float32)
+    heads = mix_ref.shape[1] // HD
+    rstds = []
+    for tile in range(tiles):
+        h0 = jnp.dot(emb_ref[...], tok_ref[tile], preferred_element_type=jnp.float32) + pos_ref[...].astype(jnp.float32)
+        h0_ref[tile] = h0
+        rstds.append(norm_rows(h0)[1])
+
+    for k, copy in enumerate(z_copies):
+        copy.wait_recv()
+        slot = lax.rem(level + levels - k - 1, levels) * LO + lane
+        y_copies.append(send(all_ref.at[slot], all_ref.at[slot], (fys, fyr), k + 1, beside))
+        c_copies.append(send(all_ref.at[slot], all_ref.at[slot], (fcs, fcr), k + 1, mate))
+    for k in range(levels):
+        y_copies[k].wait_recv()
+        slot = lax.rem(level + levels - k, levels) * LO + side
+        c_copies.append(send(all_ref.at[slot], all_ref.at[slot], (fcs, fcr), levels + k, mate))
+    for copy in c_copies:
+        copy.wait_recv()
+    for k in range(levels):
+        wy_copies[k].wait_recv()
+        slot = lax.rem(level + levels - k, levels) * LO + side
+        wc_copies.append(send(wo_ref.at[slot], wo_ref.at[slot], (wcs, wcr), levels + k, mate))
 
     def head_norm(proj, gain):
         spread = jnp.mean(proj * proj, axis=0, keepdims=True)
         return (proj * lax.rsqrt(spread + 1e-06) * gain).astype(jnp.bfloat16)
 
-    for head in range(heads):
-        query = head_norm(project(0, head), qg_ref[...])
-        key = head_norm(project(1, head), kg_ref[...])
-        value = project(2, head).astype(jnp.bfloat16)
-        scores = lax.dot_general(key, query, (((0,), (0,)), ((), ())), preferred_element_type=jnp.float32) * HD ** (-0.5)
-        expo = jnp.exp(scores - jnp.max(scores, axis=0, keepdims=True))
-        probs = (expo * (1.0 / jnp.sum(expo, axis=0, keepdims=True))).astype(jnp.bfloat16)
-        mixed = jnp.dot(value, probs, preferred_element_type=jnp.float32)
-        mix_ref[head * HD : (head + 1) * HD, :] = mixed.astype(jnp.bfloat16)
-    attn = jnp.dot(wo_ref[...], mix_ref[...], preferred_element_type=jnp.float32)
-    center, rstd1 = norm_rows(h0 + gate_ref[...] * attn)
-    final = (center * rstd1).astype(jnp.bfloat16)
-    eps_ref[0] = jnp.dot(out_w_ref[...], final, preferred_element_type=jnp.float32).astype(jnp.bfloat16)
-
-
-def denoise(chosen, embed_w, pos_embed, shift_vec, scale_vec, gate_vec, wq, wk, wv, wo, q_gain, k_gain, out_w):
+    last = token_count + token_values
+
+    @pl.loop(0, heads)
+    def _(head):
+        blocks = [all_ref[pl.ds(head * group, group), kind].reshape(HD, fold_ref.shape[2]) for kind in range(3)]
+        for tile in range(tiles):
+            parts3 = []
+            for block in blocks:
+                own = jnp.dot(block[:, token_count:last], tok_ref[tile], preferred_element_type=jnp.float32)
+                proj = (own + block[:, :token_count].astype(jnp.float32)) * rstds[tile]
+                parts3.append(proj + block[:, last : last + 1].astype(jnp.float32))
+            query = head_norm(parts3[0], qg_ref[...])
+            key = head_norm(parts3[1], kg_ref[...])
+            value = parts3[2].astype(jnp.bfloat16)
+            scores = lax.dot_general(key, query, (((0,), (0,)), ((), ())), preferred_element_type=jnp.float32) * HD ** (-0.5)
+            expo = jnp.exp(scores - jnp.max(scores, axis=0, keepdims=True))
+            probs = (expo * (1.0 / jnp.sum(expo, axis=0, keepdims=True))).astype(jnp.bfloat16)
+            mixed = jnp.dot(value, probs, preferred_element_type=jnp.float32)
+            mix_ref[tile, pl.ds(pl.multiple_of(head * HD, HD), HD), :] = mixed.astype(jnp.bfloat16)
+
+    for copy in wc_copies:
+        copy.wait_recv()
+    wo_t = wo_ref[...].reshape(-1, wo_ref.shape[2])
+    for tile in range(tiles):
+        attn = jnp.dot(wo_t, mix_ref[tile], preferred_element_type=jnp.float32)
+        center, rstd1 = norm_rows(h0_ref[tile] + gate_ref[...] * attn)
+        final = (center * rstd1).astype(jnp.bfloat16)
+        eps_ref[tile] = jnp.dot(out_w_ref[...], final, preferred_element_type=jnp.float32).astype(jnp.bfloat16)
+    for copy in z_copies + y_copies + c_copies + wy_copies + wc_copies:
+        copy.wait_send()
+
+
+def denoise(chosen, embed_w, pos_embed, local_mod, wq, wk, wv, wo, q_gain, k_gain, out_w):
     parts = lax.axis_size("tile")
+    levels = parts // LO
     tiles, token_values, token_count = chosen.shape
     width = embed_w.shape[1]
     inner = wq.shape[1]
@@ -112,25 +240,49 @@
     rows = wq.shape[0]
     stacked = jnp.stack([wq, wk, wv], axis=1).reshape(rows, 3, parts, per)
     chunks = jnp.transpose(stacked, (2, 0, 1, 3)).reshape(parts, rows, 3 * per)
-    mine = lax.all_to_all(chunks, "tile", 0, 0, tiled=True).reshape(width, 3 * per)
-    wo_t = lax.all_gather(wo.T, "tile", axis=0, tiled=True)
+    wo_t = wo.T
+    mod_rows = jnp.broadcast_to(local_mod, (8, local_mod.shape[1]))
+    in_vmem = pl.BlockSpec(memory_space=pltpu.VMEM)
+    mods, mine, line = pl.pallas_call(
+        functools.partial(spread_kernel, parts),
+        out_shape=(
+            jax.ShapeDtypeStruct((parts,) + mod_rows.shape, jnp.float32),
+            jax.ShapeDtypeStruct(chunks.shape, jnp.bfloat16),
+            jax.ShapeDtypeStruct((levels,) + wo_t.shape, jnp.bfloat16),
+        ),
+        in_specs=[in_vmem] * 3,
+        out_specs=(in_vmem,) * 3,
+        scratch_shapes=pair(parts) + pair(parts) + pair(levels),
+        compiler_params=pltpu.CompilerParams(collective_id=0, has_side_effects=True, vmem_limit_bytes=32 * 1024 * 1024),
+    )(mod_rows, chunks, wo_t)
+    mine = mine.reshape(width, 3 * per)
+    modulation = mods[:, 0].reshape(1, -1)
+    shift_vec = modulation[:, :width]
+    scale_vec = modulation[:, width : 2 * width]
+    gate_vec = modulation[:, 2 * width :]
     folded = jnp.concatenate([centered(pos_embed), centered(embed_w)], axis=0) * (1.0 + scale_vec)
     pad = -(token_count + token_values + 1) % HD
     left = jnp.concatenate([folded, shift_vec, jnp.zeros((pad, width), jnp.float32)], axis=0).astype(jnp.bfloat16)
     fold = lax.dot_general(mine, left, (((0,), (1,)), ((), ())), preferred_element_type=jnp.float32)
-    fold = fold.astype(jnp.bfloat16).reshape(1, 3, per, left.shape[0])
-    fold_all = lax.all_gather(fold, "tile", axis=0, tiled=True)
-    args = (chosen, fold_all, wo_t, embed_w.T, pos_embed.T, gate_vec.reshape(-1, 1), out_w.T, q_gain.reshape(-1, 1), k_gain.reshape(-1, 1))
-    whole = [pl.BlockSpec(memory_space=pltpu.VMEM)] * (len(args) - 1)
-    block = pl.BlockSpec((1, token_values, token_count), lambda i: (i, 0, 0))
+    fold = fold.astype(jnp.bfloat16).reshape(3, per, left.shape[0])
+    args = (chosen, fold, line, embed_w.T, pos_embed.T, gate_vec.reshape(-1, 1), out_w.T, q_gain.reshape(-1, 1), k_gain.reshape(-1, 1))
     return pl.pallas_call(
-        denoise_kernel,
-        grid=(tiles,),
+        functools.partial(denoise_kernel, parts),
         out_shape=jax.ShapeDtypeStruct(chosen.shape, jnp.bfloat16),
-        in_specs=[block] + whole,
-        out_specs=block,
-        scratch_shapes=[pltpu.VMEM((inner, token_count), jnp.bfloat16)],
-        compiler_params=pltpu.CompilerParams(vmem_limit_bytes=48 * 1024 * 1024),
+        in_specs=[in_vmem] * len(args),
+        out_specs=in_vmem,
+        scratch_shapes=[
+            pltpu.VMEM((parts,) + fold.shape, jnp.bfloat16),
+            pltpu.VMEM((parts,) + wo_t.shape, jnp.bfloat16),
+            pltpu.VMEM((tiles, width, token_count), jnp.float32),
+            pltpu.VMEM((tiles, inner, token_count), jnp.bfloat16),
+        ]
+        + pair(levels)
+        + pair(levels)
+        + pair(2 * levels)
+        + pair(levels)
+        + pair(2 * levels),
+        compiler_params=pltpu.CompilerParams(collective_id=1, has_side_effects=True, vmem_limit_bytes=56 * 1024 * 1024),
     )(*args)
 
 
@@ -155,24 +307,17 @@
     channels, band_rows, band_cols = latent.shape
     tile_side = band_rows // PATCH
     tiles_here = band_cols // band_rows
-    width = embed_w.shape[1]
     step_now = timestep[0].astype(jnp.float32)
     cos_now, sin_now = plan(step_now)
     cos_prev, sin_prev = plan(step_now - STRIDE)
     time_code = time_features(step_now, mod_w.shape[0])
     local_mod = jnp.dot(time_code, mod_w, preferred_element_type=jnp.float32)
-    modulation = lax.all_gather(local_mod, "tile", axis=1, tiled=True)
-    shift_vec = modulation[:, :width]
-    scale_vec = modulation[:, width : 2 * width]
-    gate_vec = modulation[:, 2 * width :]
     tile_tokens = band_tiles(latent.astype(jnp.bfloat16), tile_side)
     order_in = jnp.cumsum(cloudy) - cloudy
     weights_all = (
         embed_w,
         pos_embed,
-        shift_vec,
-        scale_vec,
-        gate_vec,
+        local_mod,
         wq,
         wk,
         wv,

time: 209 us -> 183 us (0.88)
  Pallas kernels: 27 us -> 127 us
  waiting for transfers between devices: 83 us -> 2.29 us
  blocking collectives: 27.8 us -> 0 us
  between operations: 15.5 us -> 2.13 us
  starting transfers between devices: 12.1 us -> 4.54 us
  other arithmetic: 7.23 us -> 13.2 us
    pallas_call x1 -> x2, Pallas kernels: 27 us -> 127 us  [the longest x1 75.7 us: denoise(): pl.pallas_call(functools.partial(denoise_kernel, parts), out_shape=jax.Sh...]
    all_gather x2 -> x0, waiting for transfers between devices: 80.2 us -> none  [the longest x1 52.1 us: denoise(): wo_t = lax.all_gather(wo.T, 'tile', axis=0, tiled=True)]
    all_gather x1 -> x0, blocking collectives: 27.8 us -> none  [on_device(): modulation = lax.all_gather(local_mod, 'tile', axis=1, tiled=True)]
    all_to_all x1 -> x0, starting transfers between devices: 7.48 us -> none  [denoise(): lax.all_to_all(chunks, 'tile', 0, 0, tiled=True).reshape(width, 3 * per)]
    sub x2, other arithmetic: 0.35 us -> 2.68 us  [centered(): return values - jnp.mean(values, axis=-1, keepdims=True)]
  transfers between devices with their start and end apart: 5 -> 2, of which waited for: 3 -> 1; matrix products, arithmetic and copies ran while one was open for 8% -> 0% of each run, Pallas kernels for 0% -> 0%
where the time goes in v2:
time: 183 us
  Pallas kernels  127 us (69%)
  local copies, waits for them, and re-layouts  25.9 us (14%)
  other arithmetic  13.2 us (7%)
  matrix products  7.58 us (4%)
  starting transfers between devices  4.54 us (2%)
  waiting for transfers between devices  2.29 us (1%)
  between operations  2.13 us (1%)
    pallas_call x1, Pallas kernels, denoise(): pl.pallas_call(functools.partial(denoise_kernel, parts), out_shape=jax.Sh...  75.7 us
    pallas_call x1, Pallas kernels, denoise(): pl.pallas_call(functools.partial(spread_kernel, parts), out_shape=(jax.Sh...  51.5 us
    unnamed x44, local copies, waits for them, and re-layouts  13.7 us
    dot_general x9, matrix products, on_device(): jnp.einsum('oc,chw->ohw', conv_w[3 * row_shift + col_shift], window, prec...  5.8 us
  transfers between devices with their start and end apart: 2, of which 1 were waited for; matrix products, arithmetic and copies ran while one was open for 0% of the time, Pallas kernels for 0%

profile of v2, /device:TPU:1, one launch (start us, length us, event | category | flops | bytes accessed | tf_op | source)
XLA Modules:
  0.0 182.9 jit_solution(1930839177051902547)
XLA Ops:
  1.4 1.1 copy.81
  2.5 1.1 copy.82
  3.7 1.1 copy.83
  6.2 51.5 %shard_map.167 = (f32[16,8,384]{2,1,0:T(8,128)S(1)}, bf16[16,128,192]{2,1,0:T(8,128)(2,1)S(1)}, bf16[4,128,1024]{2,1,0:T(8,128)(2,1)S(1)}) custom-call(f32[8,384]{1,0:T(8,128)S(1)} %broadcast_in_dim.93.mod_ref, bf16[16,128,192]{2,1,0:T(8,128)(2,1)S(1)} %copy.86.chunk_ref, bf16[128,1024]{1,0:T(8,128)(2,1)S(1)} %bitcast.83), custom_call_target="tpu_custom_call" | custom-call | tf_op jit(solution)/shard_map/pallas_call | solution.py:246
  57.7 1.0 copy-done.1
  60.6 1.5 convert_reduce_fusion
  62.1 2.3 %copy.88 = bf16[256,2048]{0,1:T(8,128)(2,1)} copy(bf16[256,2048]{1,0:T(8,128)(2,1)} %param.21) | data formatting | bytes 2097152 | tf_op args[5]
  64.6 1.0 copy.87
  65.8 1.5 convert_subtract_fusion
  67.3 1.1 convert_subtract_fusion.1
  69.5 1.1 copy.79
  71.2 0.9 copy.80
  72.1 1.3 copy.90.gate_ref
  73.4 2.0 %copy.89 = bf16[2048,128]{0,1:T(8,128)(2,1)} copy(bf16[2048,128]{1,0:T(8,128)(2,1)} %param.30) | data formatting | bytes 1048576 | tf_op args[14]
  75.5 0.7 copy.91.qg_ref
  76.2 0.7 copy.92.kg_ref
  78.2 1.6 gather_fusion
  79.8 1.4 broadcast_select_fusion.2.tok_ref
  81.2 1.6 fusion
  82.8 1.6 fusion.9
  84.4 75.7 %shard_map.168 = bf16[3,128,256]{2,1,0:T(8,128)(2,1)} custom-call(bf16[3,128,256]{2,1,0:T(8,128)(2,1)} %broadcast_select_fusion.2.tok_ref, bf16[3,64,512]{2,1,0:T(8,128)(2,1)} %bitcast.94, bf16[4,128,1024]{2,1,0:T(8,128)(2,1)} %copy-done.1, bf16[2048,128]{1,0:T(8,128)(2,1)} %bitcast.89, bf16[2048,256]{1,0:T(8,128)(2,1)} %bitcast.86, ...), custom_call_target="tpu_custom_call" | custom-call | tf_op jit(solution)/shard_map/pallas_call | solution.py:269
  160.1 1.6 gather_fusion.1
  162.3 1.1 multiply_bitcast_fusion
  163.4 1.1 copy.94
  165.6 1.7 copy_select_fusion
  167.3 2.1 %collective-permute-start = (f32[32,1,128]{2,0,1:T(8,128)S(1)}, f32[32,1,128]{2,0,1:T(8,128)S(1)}, u32[]{:S(2)}, u32[]{:S(2)}) collective-permute-start(f32[32,1,128]{2,0,1:T(8,128)S(1)} %get-tuple-element.19), channel_id=1, source_target_pairs={{0,1},{1,2},{2,3},{3,4},{4,5},{5,6},{6,7},{7,8},{8,9},{9,10},{10,1... | collective-permute-start | bytes 49160 | tf_op jit(solution)/shard_map/ppermute | solution.py:23
  169.4 2.5 %collective-permute-start.1 = (f32[32,1,128]{2,0,1:T(8,128)S(1)}, f32[32,1,128]{2,0,1:T(8,128)S(1)}, u32[]{:S(2)}, u32[]{:S(2)}) collective-permute-start(f32[32,1,128]{2,0,1:T(8,128)S(1)} %get-tuple-element.20), channel_id=1, source_target_pairs={{1,0},{2,1},{3,2},{4,3},{5,4},{6,5},{7,6},{8,7},{9,8},{10,9},{11,1... | collective-permute-start | bytes 49160 | tf_op jit(solution)/shard_map/ppermute | solution.py:26
  172.1 2.3 %collective-permute-done.1 = f32[32,1,128]{2,0,1:T(8,128)S(1)} collective-permute-done((f32[32,1,128]{2,0,1:T(8,128)S(1)}, f32[32,1,128]{2,0,1:T(8,128)S(1)}, u32[]{:S(2)}, u32[]{:S(2)}) %collective-permute-start.1) | collective-permute-done | bytes 16416 | tf_op jit(solution)/shard_map/ppermute | solution.py:26
  176.6 0.7 convolution_add_fusion.5
  179.8 0.9 fusion.28
  180.7 1.1 copy.100
  181.8 1.1 copy.99
  (77 shorter events, 12.5 us)
Async XLA Ops:
  0.6 5.4 %copy-start = (bf16[256,384]{1,0:T(8,128)(2,1)S(1)}, bf16[256,384]{1,0:T(8,128)(2,1)}, u32[]{:S(2)}) copy-start(bf16[256,384]{1,0:T(8,128)(2,1)} %param.23) | copy-start | bytes 589828
  4.9 1.0 copy-start.8
  5.0 53.8 %copy-start.16 = (s32[4]{0:T(128)S(1)}, s32[4]{0:T(128)}, u32[]{:S(2)}) copy-start(s32[4]{0:T(128)} %param.19) | copy-start | bytes 52
  57.7 1.0 copy-start.1
  59.5 0.5 copy-start.10
  60.6 3.9 %copy-start.4 = (bf16[128,2048]{1,0:T(8,128)(2,1)S(1)}, bf16[128,2048]{1,0:T(8,128)(2,1)}, u32[]{:S(2)}) copy-start(bf16[128,2048]{1,0:T(8,128)(2,1)} %param.22) | copy-start | bytes 1572868
  62.1 3.7 %copy-start.2 = (bf16[256,2048]{1,0:T(8,128)(2,1)S(1)}, bf16[256,2048]{1,0:T(8,128)(2,1)}, u32[]{:S(2)}) copy-start(bf16[256,2048]{1,0:T(8,128)(2,1)} %param.21) | copy-start | bytes 3145732
  67.3 1.7 copy-start.5
  71.2 4.3 %copy-start.14 = (f32[128]{0:T(128)S(1)}, f32[128]{0:T(128)}, u32[]{:S(2)}) copy-start(f32[128]{0:T(128)} %param.28) | copy-start | bytes 1540
  71.2 5.0 %copy-start.15 = (f32[128]{0:T(128)S(1)}, f32[128]{0:T(128)}, u32[]{:S(2)}) copy-start(f32[128]{0:T(128)} %param.29) | copy-start | bytes 1540
  72.1 9.1 %copy-start.3 = (f32[256,2048]{1,0:T(8,128)S(1)}, f32[256,2048]{1,0:T(8,128)}, u32[]{:S(2)}) copy-start(f32[256,2048]{1,0:T(8,128)} %convert_subtract_fusion) | copy-start | bytes 6291460
  81.2 1.6 copy-start.13
  160.1 2.2 %copy-start.11 = (pred[4]{0:T(512)(128)(4,1)S(1)}, pred[4]{0:T(512)(128)(4,1)}, u32[]{:S(2)}) copy-start(pred[4]{0:T(512)(128)(4,1)} %copy-done.10) | copy-start | bytes 16
  160.1 2.2 %copy-start.12 = (pred[4]{0:T(512)(128)(4,1)S(1)}, pred[4]{0:T(512)(128)(4,1)}, u32[]{:S(2)}) copy-start(pred[4]{0:T(512)(128)(4,1)} %get-tuple-element.16) | copy-start | bytes 16
  164.6 1.0 copy-start.6
  165.6 9.2 %copy-start.9 = (f32[9,32,32]{2,1,0:T(8,128)S(1)}, f32[9,32,32]{2,1,0:T(8,128)}, u32[]{:S(2)}) copy-start(f32[9,32,32]{2,1,0:T(8,128)} %param.31) | copy-start | bytes 110596
  167.3 4.8 %collective-permute-start = (f32[32,1,128]{2,0,1:T(8,128)S(1)}, f32[32,1,128]{2,0,1:T(8,128)S(1)}, u32[]{:S(2)}, u32[]{:S(2)}) collective-permute-start(f32[32,1,128]{2,0,1:T(8,128)S(1)} %get-tuple-element.19), channel_id=1, source_target_pairs={{0,1},{1,2},{2,3},{3,4},{4,5},{5,6},{6,7},{7,8},{8,9},{9,10},{10,1... | collective-permute-start | bytes 49160 | tf_op jit(solution)/shard_map/ppermute | solution.py:23
  169.4 5.1 %collective-permute-start.1 = (f32[32,1,128]{2,0,1:T(8,128)S(1)}, f32[32,1,128]{2,0,1:T(8,128)S(1)}, u32[]{:S(2)}, u32[]{:S(2)}) collective-permute-start(f32[32,1,128]{2,0,1:T(8,128)S(1)} %get-tuple-element.20), channel_id=1, source_target_pairs={{1,0},{2,1},{3,2},{4,3},{5,4},{6,5},{7,6},{8,7},{9,8},{10,9},{11,1... | collective-permute-start | bytes 49160 | tf_op jit(solution)/shard_map/ppermute | solution.py:26
  178.5 1.3 copy-start.7

commit v3 on v2

v3 whole, which is shorter than its diff:
```python
import functools
import math

import jax
import jax.numpy as jnp
from jax import lax
from jax.experimental import pallas as pl
from jax.experimental.pallas import tpu as pltpu
from jax.sharding import PartitionSpec as P

HD = 128
PATCH = 2
MAXOWN = 3
TSTEPS = 1000
STRIDE = 20


def padded_2(block, sides, width):
    for axis, dim in sides:
        count = lax.axis_size(axis)
        forward = [(i, i + 1) for i in range(count - 1)]
        backward = [(target, source) for source, target in forward]
        low = lax.ppermute(
            lax.slice_in_dim(block, block.shape[dim] - width, None, axis=dim), axis, forward
        )
        high = lax.ppermute(lax.slice_in_dim(block, 0, width, axis=dim), axis, backward)
        block = jnp.concatenate([low, block, high], axis=dim)
    return block


def plan(step):
    theta = (step / TSTEPS + 0.008) / 1.008 * (math.pi / 2)
    return (jnp.cos(theta), jnp.sin(theta))


def time_features(step, width):
    half = width // 2
    freqs = jnp.exp(-math.log(10000.0) * jnp.arange(half, dtype=jnp.float32) / half)
    angles = step * freqs
    code = jnp.concatenate([jnp.cos(angles), jnp.sin(angles)])[None, :]
    return jax.nn.silu(code).astype(jnp.bfloat16)


def band_tiles(band, tile_side):
    channels, band_rows, band_cols = band.shape
    tiles_here = band_cols // (tile_side * PATCH)
    shaped = band.reshape(channels, tile_side, PATCH, tiles_here, tile_side, PATCH)
    return jnp.transpose(shaped, (3, 2, 5, 0, 1, 4)).reshape(
        tiles_here, PATCH * PATCH * channels, tile_side * tile_side
    )


def band_pixels(tiled, tile_side, channels):
    tiles_here = tiled.shape[0]
    shaped = tiled.reshape(tiles_here, PATCH, PATCH, channels, tile_side, tile_side)
    return jnp.transpose(shaped, (3, 4, 1, 0, 5, 2)).reshape(
        channels, tile_side * PATCH, tiles_here * tile_side * PATCH
    )


def centered(values):
    values = values.astype(jnp.float32)
    return values - jnp.mean(values, axis=-1, keepdims=True)


LO = 4


def send(src, dst, sems, slot, target):
    copy = pltpu.make_async_remote_copy(
        src_ref=src,
        dst_ref=dst,
        send_sem=sems[0].at[slot],
        recv_sem=sems[1].at[slot],
        device_id=target,
        device_id_type=pl.DeviceIdType.MESH,
    )
    copy.start()
    return copy


def pair(count):
    return [pltpu.SemaphoreType.DMA((count,)), pltpu.SemaphoreType.DMA((count,))]


def norm_rows(values):
    center = values - jnp.mean(values, axis=0, keepdims=True)
    spread = jnp.mean(center * center, axis=0, keepdims=True)
    return center, lax.rsqrt(spread + 1e-06)


def column(row):
    return jnp.broadcast_to(row, (8, row.shape[1])).T[:, 0:1]


def denoise_kernel(
    parts,
    tok_ref,
    mod_ref,
    wq_ref,
    wk_ref,
    wv_ref,
    wo_in_ref,
    emb_ref,
    pos_ref,
    out_w_ref,
    qg_ref,
    kg_ref,
    eps_ref,
    chunk_ref,
    mods_ref,
    mine_ref,
    left_ref,
    all_ref,
    wo_ref,
    h0_ref,
    mix_ref,
    ms,
    mr,
    cs,
    cr,
    fzs,
    fzr,
    fys,
    fyr,
    fcs,
    fcr,
    wzs,
    wzr,
    wys,
    wyr,
    wxs,
    wxr,
    wcs,
    wcr,
):
    me = lax.axis_index("tile")
    grp = lax.axis_index("grp")
    half = lax.rem(grp, 2)
    rest = 1 - half
    across = grp + 1 - 2 * half
    level, lane = me // LO, lax.rem(me, LO)
    levels = parts // LO
    side = lax.rem(lane + 2, LO)
    twin = lane + 1 - 2 * lax.rem(lane, 2)
    others = [lax.rem(me + k, parts) for k in range(1, parts)]
    line = [lax.rem(level + k, levels) * LO + lane for k in range(1, levels)]
    beside, mate = level * LO + side, level * LO + twin
    lane_slots = [lax.rem(level + levels - k, levels) * LO + lane for k in range(levels)]
    side_slots = [lax.rem(level + levels - k, levels) * LO + side for k in range(levels)]

    barrier = pltpu.get_barrier_semaphore()
    for target in others:
        pl.semaphore_signal(barrier, inc=1, device_id={"tile": target}, device_id_type=pl.DeviceIdType.MESH)
    pl.semaphore_signal(barrier, inc=1, device_id={"grp": across}, device_id_type=pl.DeviceIdType.MESH)

    per = wq_ref.shape[1] // parts
    for part in range(parts):
        pieces = [ref[:, part * per : (part + 1) * per] for ref in (wq_ref, wk_ref, wv_ref)]
        chunk_ref[part] = jnp.concatenate(pieces, axis=1)
    pl.semaphore_wait(barrier, parts)

    mod_copies = [send(mod_ref, mods_ref.at[me], (ms, mr), k, {"tile": t}) for k, t in enumerate(others)]
    chunk_copies = [send(chunk_ref.at[t], mine_ref.at[me], (cs, cr), k, {"tile": t}) for k, t in enumerate(others)]
    mods_ref[me] = mod_ref[...]
    mine_ref[me] = chunk_ref[me]
    wo_ref[me] = wo_in_ref[...]

    tiles, token_values, token_count = tok_ref.shape
    width = emb_ref.shape[1]
    pos = pos_ref[...].astype(jnp.float32)
    pos_t = pos.T
    rstds = []
    for tile in range(tiles):
        own = lax.dot_general(emb_ref[...], tok_ref[tile], (((0,), (0,)), ((), ())), preferred_element_type=jnp.float32)
        h0 = own + pos_t
        h0_ref[tile] = h0
        rstds.append(norm_rows(h0)[1])
    query_gain, key_gain = column(qg_ref[...]), column(kg_ref[...])
    for copy in mod_copies:
        copy.wait_recv()
    modulation = jnp.concatenate([mods_ref[part] for part in range(parts)], axis=1)
    scale = 1.0 + modulation[0:1, width : 2 * width]
    gate = modulation[:, 2 * width :].T[:, 0:1]
    last = token_count + token_values
    left_ref[:token_count] = (centered(pos) * scale).astype(jnp.bfloat16)
    left_ref[token_count:last] = (centered(emb_ref[...]) * scale).astype(jnp.bfloat16)
    left_ref[last:] = jnp.broadcast_to(modulation[0:1, :width], (left_ref.shape[0] - last, width)).astype(jnp.bfloat16)
    for copy in chunk_copies:
        copy.wait_recv()

    mine = mine_ref[...].reshape(width, 3 * per)
    fold = lax.dot_general(mine, left_ref[...], (((0,), (1,)), ((), ())), preferred_element_type=jnp.float32)
    all_ref[me] = fold.astype(jnp.bfloat16).reshape(3, per, left_ref.shape[0])

    z_copies = [send(all_ref.at[me], all_ref.at[me], (fzs, fzr), k, {"tile": t}) for k, t in enumerate(line)]
    y_copies = [send(all_ref.at[me], all_ref.at[me], (fys, fyr), 0, {"tile": beside})]
    c_copies = [send(all_ref.at[me], all_ref.at[me], (fcs, fcr), 0, {"tile": mate})]
    wz_copies = [
        send(wo_ref.at[me, half], wo_ref.at[me, half], (wzs, wzr), k, {"tile": t}) for k, t in enumerate(line)
    ]
    for k, copy in enumerate(z_copies):
        copy.wait_recv()
        block = all_ref.at[lane_slots[k + 1]]
        y_copies.append(send(block, block, (fys, fyr), k + 1, {"tile": beside}))
        c_copies.append(send(block, block, (fcs, fcr), k + 1, {"tile": mate}))
    wy_copies, wx_copies, wc_copies = [], [], []

    def pass_wo(copies, sems, slot, which, target):
        block = wo_ref.at[slot, which]
        copies.append(send(block, block, sems, len(copies), target))

    pass_wo(wy_copies, (wys, wyr), me, half, {"tile": beside})
    pass_wo(wc_copies, (wcs, wcr), me, half, {"tile": mate})
    pass_wo(wc_copies, (wcs, wcr), me, rest, {"tile": mate})
    for k in range(1, levels):
        wz_copies[k - 1].wait_recv()
        pass_wo(wy_copies, (wys, wyr), lane_slots[k], half, {"tile": beside})
        pass_wo(wx_copies, (wxs, wxr), lane_slots[k], half, {"grp": across})
        pass_wo(wc_copies, (wcs, wcr), lane_slots[k], half, {"tile": mate})
    for k in range(levels):
        y_copies[k].wait_recv()
        block = all_ref.at[side_slots[k]]
        c_copies.append(send(block, block, (fcs, fcr), levels + k, {"tile": mate}))
    for copy in c_copies:
        copy.wait_recv()

    def head_norm(proj, gain):
        spread = jnp.mean(proj * proj, axis=0, keepdims=True)
        return (proj * lax.rsqrt(spread + 1e-06) * gain).astype(jnp.bfloat16)

    group = HD // per
    heads = mix_ref.shape[1] // HD

    def attend(head):
        blocks = [all_ref[pl.ds(head * group, group), kind].reshape(HD, all_ref.shape[3]) for kind in range(3)]
        for tile in range(tiles):
            projs = []
            for block in blocks:
                own = jnp.dot(block[:, token_count:last], tok_ref[tile], preferred_element_type=jnp.float32)
                proj = (own + block[:, :token_count].astype(jnp.float32)) * rstds[tile]
                projs.append(proj + block[:, last : last + 1].astype(jnp.float32))
            query = head_norm(projs[0], query_gain)
            key = head_norm(projs[1], key_gain)
            value = projs[2].astype(jnp.bfloat16)
            scores = lax.dot_general(key, query, (((0,), (0,)), ((), ())), preferred_element_type=jnp.float32) * HD ** (-0.5)
            expo = jnp.exp(scores - jnp.max(scores, axis=0, keepdims=True))
            probs = (expo * (1.0 / jnp.sum(expo, axis=0, keepdims=True))).astype(jnp.bfloat16)
            mixed = jnp.dot(value, probs, preferred_element_type=jnp.float32)
            mix_ref[tile, pl.ds(pl.multiple_of(head * HD, HD), HD), :] = mixed.astype(jnp.bfloat16)

    pl.loop(0, heads // 4)(attend)
    for k in range(levels):
        wy_copies[k].wait_recv()
        pass_wo(wx_copies, (wxs, wxr), side_slots[k], half, {"grp": across})
        pass_wo(wc_copies, (wcs, wcr), side_slots[k], half, {"tile": mate})
    pl.loop(heads // 4, heads - heads // 4)(attend)
    for k, slot in enumerate(lane_slots[1:] + side_slots):
        wx_copies[k].wait_recv()
        pass_wo(wc_copies, (wcs, wcr), slot, rest, {"tile": mate})
    pl.loop(heads - heads // 4, heads)(attend)
    for copy in wc_copies:
        copy.wait_recv()

    wo_t = wo_ref[...].reshape(width, wo_ref.shape[3])
    for tile in range(tiles):
        attn = jnp.dot(wo_t, mix_ref[tile], preferred_element_type=jnp.float32)
        center, rstd1 = norm_rows(h0_ref[tile] + gate * attn)
        final = (center * rstd1).astype(jnp.bfloat16)
        eps = lax.dot_general(out_w_ref[...], final, (((0,), (0,)), ((), ())), preferred_element_type=jnp.float32)
        eps_ref[tile] = eps.astype(jnp.bfloat16)
    for copies in (mod_copies, chunk_copies, z_copies, y_copies, c_copies, wz_copies, wy_copies, wx_copies, wc_copies):
        for copy in copies:
            copy.wait_send()


def denoise(chosen, embed_w, pos_embed, local_mod, wq, wk, wv, wo, q_gain, k_gain, out_w):
    parts = lax.axis_size("tile")
    levels = parts // LO
    tiles, token_values, token_count = chosen.shape
    width = embed_w.shape[1]
    rows, inner = wq.shape
    per = inner // parts
    wo_t = wo.T.reshape(2, -1, inner)
    mod_rows = jnp.broadcast_to(local_mod, (8, local_mod.shape[1]))
    depth = token_count + token_values + HD
    args = (chosen, mod_rows, wq, wk, wv, wo_t, embed_w, pos_embed, out_w, q_gain.reshape(1, -1), k_gain.reshape(1, -1))
    in_vmem = pl.BlockSpec(memory_space=pltpu.VMEM)
    bf16 = jnp.bfloat16
    return pl.pallas_call(
        functools.partial(denoise_kernel, parts),
        out_shape=jax.ShapeDtypeStruct(chosen.shape, bf16),
        in_specs=[in_vmem] * len(args),
        out_specs=in_vmem,
        scratch_shapes=[
            pltpu.VMEM((parts, rows, 3 * per), bf16),
            pltpu.VMEM((parts,) + mod_rows.shape, jnp.float32),
            pltpu.VMEM((parts, rows, 3 * per), bf16),
            pltpu.VMEM((depth, width), bf16),
            pltpu.VMEM((parts, 3, per, depth), bf16),
            pltpu.VMEM((parts,) + wo_t.shape, bf16),
            pltpu.VMEM((tiles, width, token_count), jnp.float32),
            pltpu.VMEM((tiles, inner, token_count), bf16),
        ]
        + pair(parts)
        + pair(parts)
        + pair(levels)
        + pair(levels)
        + pair(2 * levels)
        + pair(levels)
        + pair(levels)
        + pair(2 * levels)
        + pair(4 * levels),
        compiler_params=pltpu.CompilerParams(collective_id=0, has_side_effects=True, vmem_limit_bytes=60 * 1024 * 1024),
    )(*args)


def on_device(
    latent,
    observed,
    noise,
    cloudy,
    timestep,
    pos_embed,
    embed_w,
    mod_w,
    wq,
    wk,
    wv,
    wo,
    q_gain,
    k_gain,
    out_w,
    conv_w,
):
    channels, band_rows, band_cols = latent.shape
    tile_side = band_rows // PATCH
    tiles_here = band_cols // band_rows
    step_now = timestep[0].astype(jnp.float32)
    cos_now, sin_now = plan(step_now)
    cos_prev, sin_prev = plan(step_now - STRIDE)
    time_code = time_features(step_now, mod_w.shape[0])
    local_mod = jnp.dot(time_code, mod_w, preferred_element_type=jnp.float32)
    tile_tokens = band_tiles(latent.astype(jnp.bfloat16), tile_side)
    order_in = jnp.cumsum(cloudy) - cloudy
    weights_all = (
        embed_w,
        pos_embed,
        local_mod,
        wq,
        wk,
        wv,
        wo,
        q_gain,
        k_gain,
        out_w,
    )
    slot_ids = jnp.arange(MAXOWN, dtype=jnp.int32)
    slot_hit = (cloudy[None, :] == 1) & (order_in[None, :] == slot_ids[:, None])
    picked = jnp.sum(
        jnp.where(slot_hit, jnp.arange(tiles_here, dtype=jnp.int32)[None, :], 0), axis=1
    )
    chosen = jnp.take(tile_tokens, picked, axis=0)
    eps_chosen = denoise(chosen, *weights_all)
    eps_back = jnp.take(eps_chosen, jnp.minimum(order_in, MAXOWN - 1), axis=0)
    eps_tiles = jnp.where(cloudy[:, None, None] == 1, eps_back, jnp.zeros_like(eps_back))
    eps_latent = band_pixels(eps_tiles.astype(jnp.float32), tile_side, channels)
    cloud_cols = jnp.repeat(cloudy, band_rows) == 1
    raw_estimate = jnp.where(
        cloud_cols[None, None, :], (latent - sin_now * eps_latent) / cos_now, observed
    )
    padded = padded_2(raw_estimate, (("tile", 1),), 1)
    padded = jnp.pad(padded, ((0, 0), (0, 0), (1, 1)))
    blended = jnp.zeros_like(raw_estimate)
    for row_shift in range(3):
        for col_shift in range(3):
            window = padded[:, row_shift : row_shift + band_rows, col_shift : col_shift + band_cols]
            blended = blended + jnp.einsum(
                "oc,chw->ohw",
                conv_w[3 * row_shift + col_shift],
                window,
                precision=lax.Precision.HIGHEST,
            )
    row_pos = jnp.arange(band_rows) % band_rows
    col_pos = jnp.arange(band_cols) % band_rows
    seam_mask = ((row_pos == 0) | (row_pos == band_rows - 1))[:, None] | (
        (col_pos == 0) | (col_pos == band_rows - 1)
    )[None, :]
    estimate = jnp.where(seam_mask[None], blended, raw_estimate)
    next_latent = cos_prev * estimate + sin_prev * noise
    return (estimate, next_latent)


def solution(mesh):
    placed = (
        P(None, ("grp", "tile"), None),
        P(None, ("grp", "tile"), None),
        P(None, ("grp", "tile"), None),
        P(("grp", "tile")),
        P("grp"),
        P(),
        P(),
        P(None, "tile"),
        P("tile", None),
        P("tile", None),
        P("tile", None),
        P(None, "tile"),
        P(),
        P(),
        P(),
        P(),
    )
    return jax.shard_map(
        on_device,
        mesh=mesh,
        in_specs=placed,
        out_specs=(P(None, ("grp", "tile"), None), P(None, ("grp", "tile"), None)),
        check_vma=False,
    )
```

time: 183 us -> 137 us (0.75); the launches traced: 183 us -> 134 us
  Pallas kernels: 127 us -> 100 us
  local copies, waits for them, and re-layouts: 25.9 us -> 12.5 us
  other arithmetic: 13.2 us -> 5.65 us
    pallas_call x1 -> x0, Pallas kernels: 51.5 us -> none  [denoise(): pl.pallas_call(functools.partial(spread_kernel, parts), out_shape=(jax.Sh...]
    pallas_call x1, Pallas kernels: 75.7 us -> 100 us  [denoise(): pl.pallas_call(functools.partial(denoise_kernel, parts), out_shape=jax.Sh...]
    unnamed x44 -> x13, local copies, waits for them, and re-layouts: 13.7 us -> 4.73 us
    reshape x4 -> x0, local copies, waits for them, and re-layouts: 3.32 us -> none  [the longest x1 1.33 us: denoise(): gate_vec.reshape(-1, 1)]
    sub x2 -> x0, other arithmetic: 2.68 us -> none  [centered(): return values - jnp.mean(values, axis=-1, keepdims=True)]
where the time goes in v3:
time: 137 us; the launch traced here: 134 us
  Pallas kernels  100 us (73%)
  local copies, waits for them, and re-layouts  12.5 us (9%)
  matrix products  5.95 us (4%)
  other arithmetic  5.65 us (4%)
  starting transfers between devices  5.46 us (4%)
  waiting for transfers between devices  2.64 us (2%)
  between operations  1.89 us (1%)
    pallas_call x1, Pallas kernels, denoise(): pl.pallas_call(functools.partial(denoise_kernel, parts), out_shape=jax.Sh...  100 us
    dot_general x9, matrix products, on_device(): jnp.einsum('oc,chw->ohw', conv_w[3 * row_shift + col_shift], window, prec...  5.8 us
    unnamed x13, local copies, waits for them, and re-layouts  4.73 us
    ppermute x1, starting transfers between devices, padded_2(): lax.ppermute(lax.slice_in_dim(block, block.shape[dim] - width, None, axis...  3.32 us
  transfers between devices with their start and end apart: 2, of which 1 were waited for; matrix products, arithmetic and copies ran while one was open for 0% of the time, Pallas kernels for 0%

profile of v3, /device:TPU:1, one launch (start us, length us, event | category | flops | bytes accessed | tf_op | source)
XLA Modules:
  0.0 134.1 jit_solution(15735057121240315594)
XLA Ops:
  0.6 0.9 reduce-window.9
  1.5 0.7 compare_and_fusion.1
  3.2 1.5 %copy.48 = bf16[32,32,128]{0,2,1:T(8,128)(2,1)S(1)} copy(f32[32,32,128]{2,1,0:T(8,128)} %param.16) | data formatting | bytes 786432 | tf_op args[0]
  4.7 1.1 copy.49
  5.9 0.5 reshape.156
  6.8 0.8 copy.51
  7.7 0.6 gather_fusion
  8.2 0.8 broadcast_select_fusion.2.tok_ref
  9.2 0.6 broadcast_in_dim.88.mod_ref
  9.8 100.0 %shard_map.167 = bf16[3,128,256]{2,1,0:T(8,128)(2,1)} custom-call(bf16[3,128,256]{2,1,0:T(8,128)(2,1)} %broadcast_select_fusion.2.tok_ref, f32[8,384]{1,0:T(8,128)} %broadcast_in_dim.88.mod_ref, bf16[128,1024]{1,0:T(8,128)(2,1)} %wq_ref.1, bf16[128,1024]{1,0:T(8,128)(2,1)} %wk_ref.1, bf16[128,1024]{1,0:T(8,128)(2,1)} %wv_ref.1, ...), custom_call_target="tpu_custom_call" | custom-call | tf_op jit(solution)/shard_map/pallas_call | solution.py:290
  109.8 1.5 %gather_fusion.1 = bf16[4,128,256]{2,1,0:T(8,128)(2,1)S(1)} fusion(bf16[3,128,256]{2,1,0:T(8,128)(2,1)} %shard_map.167, s32[1024]{0:T(1024)S(1)} %pad_clamp_fusion), kind=kCustom, calls=%fused_computation.1 | custom fusion | bytes 524304 | tf_op jit(solution)/shard_map/jit(_take)/gather | solution.py:365
  111.4 0.4 gather.12
  111.9 1.1 multiply_bitcast_fusion
  112.9 1.1 copy.53
  114.1 0.6 copy.55
  115.1 1.6 %copy_select_fusion = f32[32,32,128]{2,0,1:T(8,128)S(1)} fusion(f32[32,32,128]{2,1,0:T(8,128)} %param.17, f32[32,32,128]{2,0,1:T(8,128)S(1)} %copy.55, f32[32,32,128]{2,1,0:T(8,128)S(1)} %copy-done.1, f32[]{:T(128)S(6)} %cos.10, pred[128]{0:T(512)(128)(4,1)S(1)} %eq.73), kind=kLoop, calls=%fused_computation.37 | loop fusion | flops 393216 | bytes 2097284 | tf_op jit(solution)/shard_map/jit(_where)/select_n | solution.py:369
  116.8 3.3 %collective-permute-start = (f32[32,1,128]{2,0,1:T(8,128)S(1)}, f32[32,1,128]{2,0,1:T(8,128)S(1)}, u32[]{:S(2)}, u32[]{:S(2)}) collective-permute-start(f32[32,1,128]{2,0,1:T(8,128)S(1)} %get-tuple-element.13), channel_id=1, source_target_pairs={{0,1},{1,2},{2,3},{3,4},{4,5},{5,6},{6,7},{7,8},{8,9},{9,10},{10,1... | collective-permute-start | bytes 49160 | tf_op jit(solution)/shard_map/ppermute | solution.py:23
  120.1 2.1 %collective-permute-start.1 = (f32[32,1,128]{2,0,1:T(8,128)S(1)}, f32[32,1,128]{2,0,1:T(8,128)S(1)}, u32[]{:S(2)}, u32[]{:S(2)}) collective-permute-start(f32[32,1,128]{2,0,1:T(8,128)S(1)} %get-tuple-element.14), channel_id=1, source_target_pairs={{1,0},{2,1},{3,2},{4,3},{5,4},{6,5},{7,6},{8,7},{9,8},{10,9},{11,1... | collective-permute-start | bytes 49160 | tf_op jit(solution)/shard_map/ppermute | solution.py:26
  122.6 2.6 %collective-permute-done.1 = f32[32,1,128]{2,0,1:T(8,128)S(1)} collective-permute-done((f32[32,1,128]{2,0,1:T(8,128)S(1)}, f32[32,1,128]{2,0,1:T(8,128)S(1)}, u32[]{:S(2)}, u32[]{:S(2)}) %collective-permute-start.1) | collective-permute-done | bytes 16416 | tf_op jit(solution)/shard_map/ppermute | solution.py:26
  125.2 0.4 select_maximum_fusion
  125.6 0.7 fusion.11
  126.2 0.6 fusion.4
  126.8 0.6 convolution_add_fusion.6
  127.4 0.7 convolution_add_fusion.5
  128.1 0.6 convolution_add_fusion.4
  128.7 0.6 convolution_add_fusion.3
  129.3 0.7 convolution_add_fusion.2
  130.0 0.6 convolution_add_fusion.1
  130.5 0.4 copy-done.2
  131.0 0.9 fusion.18
  131.9 1.1 copy.58
  133.0 1.1 copy.59
  (27 shorter events, 1.5 us)
Async XLA Ops:
  0.6 8.4 %copy-start = (bf16[256,384]{1,0:T(8,128)(2,1)S(1)}, bf16[256,384]{1,0:T(8,128)(2,1)}, u32[]{:S(2)}) copy-start(bf16[256,384]{1,0:T(8,128)(2,1)} %param.23) | copy-start | bytes 589828
  5.9 1.0 copy-start.3
  114.1 1.0 copy-start.1
  116.8 8.8 %copy-start.4 = (f32[9,32,32]{2,1,0:T(8,128)S(1)}, f32[9,32,32]{2,1,0:T(8,128)}, u32[]{:S(2)}) copy-start(f32[9,32,32]{2,1,0:T(8,128)} %param.31) | copy-start | bytes 110596
  116.8 5.7 %collective-permute-start = (f32[32,1,128]{2,0,1:T(8,128)S(1)}, f32[32,1,128]{2,0,1:T(8,128)S(1)}, u32[]{:S(2)}, u32[]{:S(2)}) collective-permute-start(f32[32,1,128]{2,0,1:T(8,128)S(1)} %get-tuple-element.13), channel_id=1, source_target_pairs={{0,1},{1,2},{2,3},{3,4},{4,5},{5,6},{6,7},{7,8},{8,9},{9,10},{10,1... | collective-permute-start | bytes 49160 | tf_op jit(solution)/shard_map/ppermute | solution.py:23
  120.1 5.1 %collective-permute-start.1 = (f32[32,1,128]{2,0,1:T(8,128)S(1)}, f32[32,1,128]{2,0,1:T(8,128)S(1)}, u32[]{:S(2)}, u32[]{:S(2)}) collective-permute-start(f32[32,1,128]{2,0,1:T(8,128)S(1)} %get-tuple-element.14), channel_id=1, source_target_pairs={{1,0},{2,1},{3,2},{4,3},{5,4},{6,5},{7,6},{8,7},{9,8},{10,9},{11,1... | collective-permute-start | bytes 49160 | tf_op jit(solution)/shard_map/ppermute | solution.py:26
  129.9 1.0 copy-start.2

commit v4 on v3

--- a/solution.py
+++ b/solution.py
@@ -115,6 +115,11 @@
     wo_ref,
     h0_ref,
     mix_ref,
+    flat_ref,
+    flats_ref,
+    shift_ref,
+    ss,
+    sr,
     ms,
     mr,
     cs,
@@ -155,9 +160,10 @@
     pl.semaphore_signal(barrier, inc=1, device_id={"grp": across}, device_id_type=pl.DeviceIdType.MESH)
 
     per = wq_ref.shape[1] // parts
-    for part in range(parts):
-        pieces = [ref[:, part * per : (part + 1) * per] for ref in (wq_ref, wk_ref, wv_ref)]
-        chunk_ref[part] = jnp.concatenate(pieces, axis=1)
+    for kind, ref in enumerate((wq_ref, wk_ref, wv_ref)):
+        turned = ref[...].T
+        for part in range(parts):
+            chunk_ref[part, kind] = turned[part * per : (part + 1) * per]
     pl.semaphore_wait(barrier, parts)
 
     mod_copies = [send(mod_ref, mods_ref.at[me], (ms, mr), k, {"tile": t}) for k, t in enumerate(others)]
@@ -181,29 +187,42 @@
         copy.wait_recv()
     modulation = jnp.concatenate([mods_ref[part] for part in range(parts)], axis=1)
     scale = 1.0 + modulation[0:1, width : 2 * width]
-    gate = modulation[:, 2 * width :].T[:, 0:1]
+    gate = column(modulation[:, 2 * width :])
     last = token_count + token_values
     left_ref[:token_count] = (centered(pos) * scale).astype(jnp.bfloat16)
     left_ref[token_count:last] = (centered(emb_ref[...]) * scale).astype(jnp.bfloat16)
-    left_ref[last:] = jnp.broadcast_to(modulation[0:1, :width], (left_ref.shape[0] - last, width)).astype(jnp.bfloat16)
+    shift = jnp.broadcast_to(modulation[:, :width], (16, width)).astype(jnp.bfloat16)
     for copy in chunk_copies:
         copy.wait_recv()
 
-    mine = mine_ref[...].reshape(width, 3 * per)
-    fold = lax.dot_general(mine, left_ref[...], (((0,), (1,)), ((), ())), preferred_element_type=jnp.float32)
+    mine = jnp.concatenate([mine_ref[part].reshape(3 * per, -1) for part in range(parts)], axis=1)
+    over_width = (((1,), (1,)), ((), ()))
+    fold = lax.dot_general(mine, left_ref[...], over_width, preferred_element_type=jnp.float32)
     all_ref[me] = fold.astype(jnp.bfloat16).reshape(3, per, left_ref.shape[0])
-
     z_copies = [send(all_ref.at[me], all_ref.at[me], (fzs, fzr), k, {"tile": t}) for k, t in enumerate(line)]
     y_copies = [send(all_ref.at[me], all_ref.at[me], (fys, fyr), 0, {"tile": beside})]
     c_copies = [send(all_ref.at[me], all_ref.at[me], (fcs, fcr), 0, {"tile": mate})]
+    flat = lax.dot_general(shift, mine, over_width, preferred_element_type=jnp.float32)[0:1]
+    flat_ref[...] = jnp.zeros_like(flat_ref)
+    flat_ref[:, : 3 * per] = flat
+    flat_copies = [send(flat_ref, flats_ref.at[me], (ss, sr), k, {"tile": t}) for k, t in enumerate(others)]
+    flats_ref[me] = flat_ref[...]
+    for k, copy in enumerate(z_copies):
+        copy.wait_recv()
+        block = all_ref.at[lane_slots[k + 1]]
+        y_copies.append(send(block, block, (fys, fyr), k + 1, {"tile": beside}))
+        c_copies.append(send(block, block, (fcs, fcr), k + 1, {"tile": mate}))
     wz_copies = [
         send(wo_ref.at[me, half], wo_ref.at[me, half], (wzs, wzr), k, {"tile": t}) for k, t in enumerate(line)
     ]
-    for k, copy in enumerate(z_copies):
-        copy.wait_recv()
-        block = all_ref.at[lane_slots[k + 1]]
-        y_copies.append(send(block, block, (fys, fyr), k + 1, {"tile": beside}))
-        c_copies.append(send(block, block, (fcs, fcr), k + 1, {"tile": mate}))
+    for k in range(levels):
+        y_copies[k].wait_recv()
+        block = all_ref.at[side_slots[k]]
+        c_copies.append(send(block, block, (fcs, fcr), levels + k, {"tile": mate}))
+    for copy in flat_copies:
+        copy.wait_recv()
+    for part in range(parts):
+        shift_ref[part] = column(flats_ref[part])[: 3 * per].reshape(3, per, 1)
     wy_copies, wx_copies, wc_copies = [], [], []
 
     def pass_wo(copies, sems, slot, which, target):
@@ -218,10 +237,6 @@
         pass_wo(wy_copies, (wys, wyr), lane_slots[k], half, {"tile": beside})
         pass_wo(wx_copies, (wxs, wxr), lane_slots[k], half, {"grp": across})
         pass_wo(wc_copies, (wcs, wcr), lane_slots[k], half, {"tile": mate})
-    for k in range(levels):
-        y_copies[k].wait_recv()
-        block = all_ref.at[side_slots[k]]
-        c_copies.append(send(block, block, (fcs, fcr), levels + k, {"tile": mate}))
     for copy in c_copies:
         copy.wait_recv()
 
@@ -233,13 +248,15 @@
     heads = mix_ref.shape[1] // HD
 
     def attend(head):
-        blocks = [all_ref[pl.ds(head * group, group), kind].reshape(HD, all_ref.shape[3]) for kind in range(3)]
+        near = pl.ds(head * group, group)
+        blocks = [all_ref[near, kind].reshape(HD, last) for kind in range(3)]
+        shifts = [shift_ref[near, kind].reshape(HD, 1) for kind in range(3)]
         for tile in range(tiles):
             projs = []
-            for block in blocks:
+            for block, base in zip(blocks, shifts):
                 own = jnp.dot(block[:, token_count:last], tok_ref[tile], preferred_element_type=jnp.float32)
                 proj = (own + block[:, :token_count].astype(jnp.float32)) * rstds[tile]
-                projs.append(proj + block[:, last : last + 1].astype(jnp.float32))
+                projs.append(proj + base)
             query = head_norm(projs[0], query_gain)
             key = head_norm(projs[1], key_gain)
             value = projs[2].astype(jnp.bfloat16)
@@ -269,7 +286,7 @@
         final = (center * rstd1).astype(jnp.bfloat16)
         eps = lax.dot_general(out_w_ref[...], final, (((0,), (0,)), ((), ())), preferred_element_type=jnp.float32)
         eps_ref[tile] = eps.astype(jnp.bfloat16)
-    for copies in (mod_copies, chunk_copies, z_copies, y_copies, c_copies, wz_copies, wy_copies, wx_copies, wc_copies):
+    for copies in (flat_copies, mod_copies, chunk_copies, z_copies, y_copies, c_copies, wz_copies, wy_copies, wx_copies, wc_copies):
         for copy in copies:
             copy.wait_send()
 
@@ -282,9 +299,9 @@
     rows, inner = wq.shape
     per = inner // parts
     wo_t = wo.T.reshape(2, -1, inner)
-    mod_rows = jnp.broadcast_to(local_mod, (8, local_mod.shape[1]))
-    depth = token_count + token_values + HD
-    args = (chosen, mod_rows, wq, wk, wv, wo_t, embed_w, pos_embed, out_w, q_gain.reshape(1, -1), k_gain.reshape(1, -1))
+    depth = token_count + token_values
+    flat_width = -(-3 * per // HD) * HD
+    args = (chosen, local_mod, wq, wk, wv, wo_t, embed_w, pos_embed, out_w, q_gain.reshape(1, -1), k_gain.reshape(1, -1))
     in_vmem = pl.BlockSpec(memory_space=pltpu.VMEM)
     bf16 = jnp.bfloat16
     return pl.pallas_call(
@@ -293,15 +310,19 @@
         in_specs=[in_vmem] * len(args),
         out_specs=in_vmem,
         scratch_shapes=[
-            pltpu.VMEM((parts, rows, 3 * per), bf16),
-            pltpu.VMEM((parts,) + mod_rows.shape, jnp.float32),
-            pltpu.VMEM((parts, rows, 3 * per), bf16),
+            pltpu.VMEM((parts, 3, per, rows), bf16),
+            pltpu.VMEM((parts,) + local_mod.shape, jnp.float32),
+            pltpu.VMEM((parts, 3, per, rows), bf16),
             pltpu.VMEM((depth, width), bf16),
             pltpu.VMEM((parts, 3, per, depth), bf16),
             pltpu.VMEM((parts,) + wo_t.shape, bf16),
             pltpu.VMEM((tiles, width, token_count), jnp.float32),
             pltpu.VMEM((tiles, inner, token_count), bf16),
+            pltpu.VMEM((1, flat_width), jnp.float32),
+            pltpu.VMEM((parts, 1, flat_width), jnp.float32),
+            pltpu.VMEM((parts, 3, per, 1), jnp.float32),
         ]
+        + pair(parts)
         + pair(parts)
         + pair(parts)
         + pair(levels)

time: 137 us -> 126 us (0.920)
  Pallas kernels: 100 us -> 84 us
  starting transfers between devices: 5.46 us -> 11.2 us
    pallas_call x1, Pallas kernels: 100 us -> 84 us  [denoise(): pl.pallas_call(functools.partial(denoise_kernel, parts), out_shape=jax.Sh...]
    ppermute x1, starting transfers between devices: 3.32 us -> 9.04 us  [padded_2(): lax.ppermute(lax.slice_in_dim(block, block.shape[dim] - width, None, axis...]
where the time goes in v4:
time: 126 us; the launch traced here: 124 us
  Pallas kernels  84 us (67%)
  local copies, waits for them, and re-layouts  11.9 us (9%)
  starting transfers between devices  11.2 us (9%)
  matrix products  6.54 us (5%)
  other arithmetic  5.65 us (4%)
  waiting for transfers between devices  2.64 us (2%)
  between operations  1.89 us (2%)
    pallas_call x1, Pallas kernels, denoise(): pl.pallas_call(functools.partial(denoise_kernel, parts), out_shape=jax.Sh...  84 us
    ppermute x1, starting transfers between devices, padded_2(): lax.ppermute(lax.slice_in_dim(block, block.shape[dim] - width, None, axis...  9.04 us
    dot_general x9, matrix products, on_device(): jnp.einsum('oc,chw->ohw', conv_w[3 * row_shift + col_shift], window, prec...  5.8 us
    unnamed x13, local copies, waits for them, and re-layouts  4.73 us
    ppermute x1, waiting for transfers between devices, padded_2(): lax.ppermute(lax.slice_in_dim(block, 0, width, axis=dim), axis, backward)  2.63 us
  transfers between devices with their start and end apart: 2, of which 1 were waited for; matrix products, arithmetic and copies ran while one was open for 0% of the time, Pallas kernels for 0%

profile of v4, /device:TPU:1, one launch (start us, length us, event | category | flops | bytes accessed | tf_op | source)
XLA Modules:
  0.0 123.8 jit_solution(11035981530945578949)
XLA Ops:
  0.6 0.9 reduce-window.9
  1.5 0.7 compare_and_fusion.1
  3.2 1.5 %copy.48 = bf16[32,32,128]{0,2,1:T(8,128)(2,1)S(1)} copy(f32[32,32,128]{2,1,0:T(8,128)} %param.16) | data formatting | bytes 786432 | tf_op args[0]
  4.7 1.1 copy.49
  5.9 0.5 reshape.155
  6.8 0.8 copy.51
  7.7 0.6 gather_fusion
  8.2 0.8 broadcast_select_fusion.2.tok_ref
  9.0 0.7 fusion.46.mod_ref
  9.7 84.0 %shard_map.167 = bf16[3,128,256]{2,1,0:T(8,128)(2,1)} custom-call(bf16[3,128,256]{2,1,0:T(8,128)(2,1)} %broadcast_select_fusion.2.tok_ref, f32[1,384]{1,0:T(1,128)} %fusion.46.mod_ref, bf16[128,1024]{1,0:T(8,128)(2,1)} %wq_ref.1, bf16[128,1024]{1,0:T(8,128)(2,1)} %wk_ref.1, bf16[128,1024]{1,0:T(8,128)(2,1)} %wv_ref.1, bf16[2,64,1024]{2,1,0:T(8,128)(2,1)} %bitcast.70, ...), custom_call_target="tpu_custom_call" | custom-call | tf_op jit(solution)/shard_map/pallas_call | solution.py:307
  93.7 1.5 %gather_fusion.1 = bf16[4,128,256]{2,1,0:T(8,128)(2,1)S(1)} fusion(bf16[3,128,256]{2,1,0:T(8,128)(2,1)} %shard_map.167, s32[1024]{0:T(1024)S(1)} %pad_clamp_fusion), kind=kCustom, calls=%fused_computation.1 | custom fusion | bytes 524304 | tf_op jit(solution)/shard_map/jit(_take)/gather | solution.py:386
  95.4 0.4 gather.12
  95.8 1.1 multiply_bitcast_fusion
  96.9 1.1 copy.53
  98.1 0.6 copy.55
  99.1 1.6 %copy_select_fusion = f32[32,32,128]{2,0,1:T(8,128)S(1)} fusion(f32[32,32,128]{2,1,0:T(8,128)} %param.17, f32[32,32,128]{2,0,1:T(8,128)S(1)} %copy.55, f32[32,32,128]{2,1,0:T(8,128)S(1)} %copy-done.1, f32[]{:T(128)S(6)} %cos.10, pred[128]{0:T(512)(128)(4,1)S(1)} %eq.73), kind=kLoop, calls=%fused_computation.36 | loop fusion | flops 393216 | bytes 2097284 | tf_op jit(solution)/shard_map/jit(_where)/select_n | solution.py:390
  100.8 9.0 %collective-permute-start = (f32[32,1,128]{2,0,1:T(8,128)S(1)}, f32[32,1,128]{2,0,1:T(8,128)S(1)}, u32[]{:S(2)}, u32[]{:S(2)}) collective-permute-start(f32[32,1,128]{2,0,1:T(8,128)S(1)} %get-tuple-element.13), channel_id=1, source_target_pairs={{0,1},{1,2},{2,3},{3,4},{4,5},{5,6},{6,7},{7,8},{8,9},{9,10},{10,1... | collective-permute-start | bytes 49160 | tf_op jit(solution)/shard_map/ppermute | solution.py:23
  109.8 2.1 %collective-permute-start.1 = (f32[32,1,128]{2,0,1:T(8,128)S(1)}, f32[32,1,128]{2,0,1:T(8,128)S(1)}, u32[]{:S(2)}, u32[]{:S(2)}) collective-permute-start(f32[32,1,128]{2,0,1:T(8,128)S(1)} %get-tuple-element.14), channel_id=1, source_target_pairs={{1,0},{2,1},{3,2},{4,3},{5,4},{6,5},{7,6},{8,7},{9,8},{10,9},{11,1... | collective-permute-start | bytes 49160 | tf_op jit(solution)/shard_map/ppermute | solution.py:26
  112.2 2.6 %collective-permute-done.1 = f32[32,1,128]{2,0,1:T(8,128)S(1)} collective-permute-done((f32[32,1,128]{2,0,1:T(8,128)S(1)}, f32[32,1,128]{2,0,1:T(8,128)S(1)}, u32[]{:S(2)}, u32[]{:S(2)}) %collective-permute-start.1) | collective-permute-done | bytes 16416 | tf_op jit(solution)/shard_map/ppermute | solution.py:26
  114.9 0.4 select_maximum_fusion
  115.2 0.7 fusion.11
  115.9 0.6 fusion.4
  116.5 0.6 convolution_add_fusion.6
  117.1 0.7 convolution_add_fusion.5
  117.8 0.6 convolution_add_fusion.4
  118.4 0.6 convolution_add_fusion.3
  118.9 0.7 convolution_add_fusion.2
  119.6 0.6 convolution_add_fusion.1
  120.2 0.4 copy-done.2
  120.7 0.9 fusion.18
  121.5 1.1 copy.58
  122.7 1.1 copy.59
  (26 shorter events, 1.4 us)
Async XLA Ops:
  0.6 8.4 %copy-start = (bf16[256,384]{1,0:T(8,128)(2,1)S(1)}, bf16[256,384]{1,0:T(8,128)(2,1)}, u32[]{:S(2)}) copy-start(bf16[256,384]{1,0:T(8,128)(2,1)} %param.23) | copy-start | bytes 589828
  5.9 1.0 copy-start.3
  98.0 1.0 copy-start.1
  100.7 14.5 %copy-start.4 = (f32[9,32,32]{2,1,0:T(8,128)S(1)}, f32[9,32,32]{2,1,0:T(8,128)}, u32[]{:S(2)}) copy-start(f32[9,32,32]{2,1,0:T(8,128)} %param.31) | copy-start | bytes 110596
  100.8 11.5 %collective-permute-start = (f32[32,1,128]{2,0,1:T(8,128)S(1)}, f32[32,1,128]{2,0,1:T(8,128)S(1)}, u32[]{:S(2)}, u32[]{:S(2)}) collective-permute-start(f32[32,1,128]{2,0,1:T(8,128)S(1)} %get-tuple-element.13), channel_id=1, source_target_pairs={{0,1},{1,2},{2,3},{3,4},{4,5},{5,6},{6,7},{7,8},{8,9},{9,10},{10,1... | collective-permute-start | bytes 49160 | tf_op jit(solution)/shard_map/ppermute | solution.py:23
  109.8 5.1 %collective-permute-start.1 = (f32[32,1,128]{2,0,1:T(8,128)S(1)}, f32[32,1,128]{2,0,1:T(8,128)S(1)}, u32[]{:S(2)}, u32[]{:S(2)}) collective-permute-start(f32[32,1,128]{2,0,1:T(8,128)S(1)} %get-tuple-element.14), channel_id=1, source_target_pairs={{1,0},{2,1},{3,2},{4,3},{5,4},{6,5},{7,6},{8,7},{9,8},{10,9},{11,1... | collective-permute-start | bytes 49160 | tf_op jit(solution)/shard_map/ppermute | solution.py:26
  119.6 1.0 copy-start.2

commit v5 on v4

--- a/solution.py
+++ b/solution.py
@@ -392,16 +392,11 @@
     )
     padded = padded_2(raw_estimate, (("tile", 1),), 1)
     padded = jnp.pad(padded, ((0, 0), (0, 0), (1, 1)))
-    blended = jnp.zeros_like(raw_estimate)
-    for row_shift in range(3):
-        for col_shift in range(3):
-            window = padded[:, row_shift : row_shift + band_rows, col_shift : col_shift + band_cols]
-            blended = blended + jnp.einsum(
-                "oc,chw->ohw",
-                conv_w[3 * row_shift + col_shift],
-                window,
-                precision=lax.Precision.HIGHEST,
-            )
+    windows = jnp.concatenate(
+        [padded[:, a : a + band_rows, b : b + band_cols] for a in range(3) for b in range(3)], axis=0
+    )
+    taps = jnp.transpose(conv_w, (1, 0, 2)).reshape(channels, -1)
+    blended = jnp.einsum("ok,khw->ohw", taps, windows, precision=lax.Precision.HIGHEST)
     row_pos = jnp.arange(band_rows) % band_rows
     col_pos = jnp.arange(band_cols) % band_rows
     seam_mask = ((row_pos == 0) | (row_pos == band_rows - 1))[:, None] | (

time: 126 us -> 124 us (0.984)
  matrix products: 6.54 us -> 4.17 us
    dot_general x9 -> x1, matrix products: 5.8 us -> 3.44 us  [on_device(): jnp.einsum('ok,khw->ohw', taps, windows, precision=lax.Precision.HIGHEST)]
    unnamed x13 -> x19, local copies, waits for them, and re-layouts: 4.73 us -> 4.45 us
where the time goes in v5:
time: 124 us; the launch traced here: 121 us
  Pallas kernels  84 us (68%)
  local copies, waits for them, and re-layouts  11.9 us (10%)
  starting transfers between devices  11 us (9%)
  other arithmetic  5.74 us (5%)
  matrix products  4.17 us (3%)
  waiting for transfers between devices  2.52 us (2%)
  between operations  1.88 us (2%)
    pallas_call x1, Pallas kernels, denoise(): pl.pallas_call(functools.partial(denoise_kernel, parts), out_shape=jax.Sh...  84 us
    ppermute x1, starting transfers between devices, padded_2(): lax.ppermute(lax.slice_in_dim(block, block.shape[dim] - width, None, axis...  8.9 us
    unnamed x19, local copies, waits for them, and re-layouts  4.45 us
    dot_general x1, matrix products, on_device(): jnp.einsum('ok,khw->ohw', taps, windows, precision=lax.Precision.HIGHEST)  3.44 us
    ppermute x1, waiting for transfers between devices, padded_2(): lax.ppermute(lax.slice_in_dim(block, 0, width, axis=dim), axis, backward)  2.52 us
  transfers between devices with their start and end apart: 2, of which 1 were waited for; matrix products, arithmetic and copies ran while one was open for 0% of the time, Pallas kernels for 0%

profile of v5, /device:TPU:1, one launch (start us, length us, event | category | flops | bytes accessed | tf_op | source)
XLA Modules:
  0.0 121.3 jit_solution(14890173114392780746)
XLA Ops:
  0.7 0.9 reduce-window.9
  1.5 0.7 compare_and_fusion.1
  2.2 0.1 select_reduce_fusion
  3.2 1.5 %copy.52 = bf16[32,32,128]{0,2,1:T(8,128)(2,1)S(1)} copy(f32[32,32,128]{2,1,0:T(8,128)} %param.16) | data formatting | bytes 786432 | tf_op args[0]
  4.7 1.1 copy.53
  5.9 0.5 reshape.158
  6.4 0.1 copy.54
  6.6 0.9 copy.55
  7.4 0.6 gather_fusion
  8.0 0.8 broadcast_select_fusion.2.tok_ref
  8.8 0.7 fusion.12.mod_ref
  9.5 84.0 %shard_map.167 = bf16[3,128,256]{2,1,0:T(8,128)(2,1)} custom-call(bf16[3,128,256]{2,1,0:T(8,128)(2,1)} %broadcast_select_fusion.2.tok_ref, f32[1,384]{1,0:T(1,128)} %fusion.12.mod_ref, bf16[128,1024]{1,0:T(8,128)(2,1)} %wq_ref.1, bf16[128,1024]{1,0:T(8,128)(2,1)} %wk_ref.1, bf16[128,1024]{1,0:T(8,128)(2,1)} %wv_ref.1, bf16[2,64,1024]{2,1,0:T(8,128)(2,1)} %bitcast.37, ...), custom_call_target="tpu_custom_call" | custom-call | tf_op jit(solution)/shard_map/pallas_call | solution.py:307
  93.5 1.5 %gather_fusion.1 = bf16[4,128,256]{2,1,0:T(8,128)(2,1)S(1)} fusion(bf16[3,128,256]{2,1,0:T(8,128)(2,1)} %shard_map.167, s32[1024]{0:T(1024)S(1)} %get-tuple-element.20), kind=kCustom, calls=%fused_computation.1 | custom fusion | bytes 524304 | tf_op jit(solution)/shard_map/jit(_take)/gather | solution.py:386
  95.0 0.2 copy.56
  95.2 0.4 gather.12
  95.6 1.1 multiply_bitcast_fusion
  96.7 1.1 copy.57
  97.8 0.6 copy.59
  98.5 0.1 eq.73
  98.6 1.6 %copy_select_fusion = f32[32,32,128]{2,0,1:T(8,128)S(1)} fusion(f32[32,32,128]{2,1,0:T(8,128)} %param.17, f32[32,32,128]{2,0,1:T(8,128)S(1)} %copy.59, f32[32,32,128]{2,1,0:T(8,128)S(1)} %copy-done.1, f32[]{:T(128)S(6)} %cos.10, pred[128]{0:T(512)(128)(4,1)S(1)} %eq.73), kind=kLoop, calls=%fused_computation.24 | loop fusion | flops 393216 | bytes 2097284 | tf_op jit(solution)/shard_map/jit(_where)/select_n | solution.py:390
  100.2 8.9 %collective-permute-start = (f32[32,1,128]{2,0,1:T(8,128)S(1)}, f32[32,1,128]{2,0,1:T(8,128)S(1)}, u32[]{:S(2)}, u32[]{:S(2)}) collective-permute-start(f32[32,1,128]{2,0,1:T(8,128)S(1)} %get-tuple-element.13), channel_id=1, source_target_pairs={{0,1},{1,2},{2,3},{3,4},{4,5},{5,6},{6,7},{7,8},{8,9},{9,10},{10,1... | collective-permute-start | bytes 49160 | tf_op jit(solution)/shard_map/ppermute | solution.py:23
  109.2 2.1 %collective-permute-start.1 = (f32[32,1,128]{2,0,1:T(8,128)S(1)}, f32[32,1,128]{2,0,1:T(8,128)S(1)}, u32[]{:S(2)}, u32[]{:S(2)}) collective-permute-start(f32[32,1,128]{2,0,1:T(8,128)S(1)} %get-tuple-element.14), channel_id=1, source_target_pairs={{1,0},{2,1},{3,2},{4,3},{5,4},{6,5},{7,6},{8,7},{9,8},{10,9},{11,1... | collective-permute-start | bytes 49160 | tf_op jit(solution)/shard_map/ppermute | solution.py:26
  111.6 0.1 copy.61
  111.7 2.5 %collective-permute-done.1 = f32[32,1,128]{2,0,1:T(8,128)S(1)} collective-permute-done((f32[32,1,128]{2,0,1:T(8,128)S(1)}, f32[32,1,128]{2,0,1:T(8,128)S(1)}, u32[]{:S(2)}, u32[]{:S(2)}) %collective-permute-start.1) | collective-permute-done | bytes 16416 | tf_op jit(solution)/shard_map/ppermute | solution.py:26
  114.2 0.4 select_maximum_fusion
  114.7 0.2 slice_dynamic-update-slice_fusion.4
  115.0 0.2 slice_dynamic-update-slice_fusion.2
  115.3 0.2 slice_dynamic-update-slice_fusion
  115.5 0.1 copy-done.2
  115.6 3.4 %fusion.4 = (f32[32,32,128]{2,0,1:T(8,128)S(1)}, f32[32,32,128]{2,0,1:T(8,128)S(1)}) fusion(f32[32,32,128]{2,1,0:T(8,128)S(1)} %copy-done.2, f32[]{:T(128)S(6)} %sin.11, f32[]{:T(128)S(6)} %cos.11, f32[32,32,128]{2,0,1:T(8,128)S(1)} %copy_select_fusion, f32[288,32,128]{2,0,1:T(8,128)S(1)} %slice_dynamic-update-slice_fusion, f32[32,288,1]{0,1,2:T(8,128)S(1)} %bitcast.38, ...), kind=kOutput, calls=%fused_computation.23 | convolution fusion | flops 453509120 | bytes 6856712 | tf_op jit(solution)/shard_map/ok,khw->ohw/dot_general | solution.py:399
  119.1 1.1 copy.64
  120.2 1.1 copy.65
  (27 shorter events, 0.5 us)
Async XLA Ops:
  0.6 8.1 %copy-start = (bf16[256,384]{1,0:T(8,128)(2,1)S(1)}, bf16[256,384]{1,0:T(8,128)(2,1)}, u32[]{:S(2)}) copy-start(bf16[256,384]{1,0:T(8,128)(2,1)} %param.23) | copy-start | bytes 589828
  0.6 5.9 %copy-start.3 = (bf16[1024,128]{1,0:T(8,128)(2,1)S(1)}, bf16[1024,128]{1,0:T(8,128)(2,1)}, u32[]{:S(2)}) copy-start(bf16[1024,128]{1,0:T(8,128)(2,1)} %param.27) | copy-start | bytes 786436
  95.6 3.0 %copy-start.1 = (f32[32,32,128]{2,1,0:T(8,128)S(1)}, f32[32,32,128]{2,1,0:T(8,128)}, u32[]{:S(2)}) copy-start(f32[32,32,128]{2,1,0:T(8,128)} %param.16) | copy-start | bytes 1572868
  96.7 14.9 %copy-start.4 = (f32[9,32,32]{2,1,0:T(8,128)S(1)}, f32[9,32,32]{2,1,0:T(8,128)}, u32[]{:S(2)}) copy-start(f32[9,32,32]{2,1,0:T(8,128)} %param.31) | copy-start | bytes 110596
  100.2 11.4 %collective-permute-start = (f32[32,1,128]{2,0,1:T(8,128)S(1)}, f32[32,1,128]{2,0,1:T(8,128)S(1)}, u32[]{:S(2)}, u32[]{:S(2)}) collective-permute-start(f32[32,1,128]{2,0,1:T(8,128)S(1)} %get-tuple-element.13), channel_id=1, source_target_pairs={{0,1},{1,2},{2,3},{3,4},{4,5},{5,6},{6,7},{7,8},{8,9},{9,10},{10,1... | collective-permute-start | bytes 49160 | tf_op jit(solution)/shard_map/ppermute | solution.py:23
  109.2 5.1 %collective-permute-start.1 = (f32[32,1,128]{2,0,1:T(8,128)S(1)}, f32[32,1,128]{2,0,1:T(8,128)S(1)}, u32[]{:S(2)}, u32[]{:S(2)}) collective-permute-start(f32[32,1,128]{2,0,1:T(8,128)S(1)} %get-tuple-element.14), channel_id=1, source_target_pairs={{1,0},{2,1},{3,2},{4,3},{5,4},{6,5},{7,6},{8,7},{9,8},{10,9},{11,1... | collective-permute-start | bytes 49160 | tf_op jit(solution)/shard_map/ppermute | solution.py:26
  114.6 1.0 copy-start.2
